TPU v7x, 32 devices: a whole 2x2x4 slice. The times are simulated.
32 devices in a mesh: dp: 16 (over z, y, core), rep: 2 (over x).
Axes of the slice: x: 2, y: 2, z: 4, core: 2. Of those that a mesh axis runs over, the one named last changes fastest.
Arguments:
- features: bfloat16 [4096, 1152], P('dp'), may hold values from -0.046875 to 0.046875
- img_weight: bfloat16 [1152, 1152], P(None, 'rep'), may hold values from -4 to 4
- text_embed: bfloat16 [4096, 1152], P('dp', 'rep'), may hold values from -0.4375 to 0.4375
- log_scale: float32 [1], replicated, may hold values from 1.6 to 2.6
- logit_bias: float32 [1], replicated, may hold values from -4 to -1
Outputs:
- image_grad: bfloat16 [4096, 1152], P('dp', 'rep')
- text_grad: bfloat16 [4096, 1152], P('dp', 'rep')
- weight_grad: bfloat16 [1152, 1152], P(None, 'rep')
All inputs are finite; a program needn't handle non-finite values.
Results may differ from a plain program's by a relative error of at most 0.017.
Values may be sent and summed in bfloat16 or wider, within the bound.
A program may use at most 64 MiB of HBM per device.

v0:
```python
import jax
import jax.numpy as jnp
from jax import lax
from jax.sharding import PartitionSpec as P

STEPS = 4


epsilon = 1e-06


def passed_along(array, axis, by):
    peers = lax.axis_size(axis)
    return lax.ppermute(array, axis, [(i, (i + by) % peers) for i in range(peers)])


def shards(features, img_weight, text_embed, log_scale, logit_bias):
    logit_scale = jnp.exp(log_scale[0])
    offset_value = logit_bias[0]
    row_count = features.shape[0]
    half_width = img_weight.shape[1]
    img_raw = jnp.dot(features, img_weight, preferred_element_type=jnp.float32)
    txt_raw = text_embed.astype(jnp.float32)
    img_sq, txt_sq = lax.psum(
        (
            jnp.sum(img_raw * img_raw, axis=1, keepdims=True),
            jnp.sum(txt_raw * txt_raw, axis=1, keepdims=True),
        ),
        "rep",
    )
    img_inv = lax.rsqrt(img_sq + epsilon)
    txt_inv = lax.rsqrt(txt_sq + epsilon)
    img_hat = img_raw * img_inv
    txt_hat = txt_raw * txt_inv
    img_bf = img_hat.astype(jnp.bfloat16)
    txt_bf = txt_hat.astype(jnp.bfloat16)
    img_use, text_span = (
        lax.all_gather(img_bf, "rep", axis=1, tiled=True),
        lax.all_gather(txt_bf, "rep", axis=1, tiled=True),
    )
    positives = jnp.eye(row_count, dtype=jnp.float32)
    grad_img = jnp.zeros(img_use.shape, jnp.float32)
    carried = jnp.zeros(text_span.shape, jnp.float32)
    for stride in range(STEPS + 1):
        if stride > 0:
            text_span = passed_along(text_span, "dp", 1)
            carried = passed_along(carried.astype(jnp.bfloat16), "dp", 1).astype(carried.dtype)
        scores = lax.dot_general(
            img_use, text_span, (((1,), (1,)), ((), ())), preferred_element_type=jnp.float32
        )
        logits = logit_scale * scores + offset_value
        sig_grad = jax.nn.sigmoid(logits)
        if stride == 0:
            sig_grad = sig_grad - positives
        grad_bf = sig_grad.astype(jnp.bfloat16)
        grad_img = grad_img + logit_scale * jnp.dot(
            grad_bf, text_span, preferred_element_type=jnp.float32
        )
        contrib = logit_scale * lax.dot_general(
            grad_bf, img_use, (((0,), (0,)), ((), ())), preferred_element_type=jnp.float32
        )
        carried = carried + contrib
    grad_txt = passed_along(carried.astype(jnp.bfloat16), "dp", -STEPS).astype(carried.dtype)
    column_start = lax.axis_index("rep") * half_width
    grad_img = lax.dynamic_slice_in_dim(grad_img, column_start, half_width, 1)
    grad_txt = lax.dynamic_slice_in_dim(grad_txt, column_start, half_width, 1)
    img_dot, txt_dot = lax.psum(
        (
            jnp.sum(img_hat * grad_img, axis=1, keepdims=True),
            jnp.sum(txt_hat * grad_txt, axis=1, keepdims=True),
        ),
        "rep",
    )
    image_grad = ((grad_img - img_hat * img_dot) * img_inv).astype(jnp.bfloat16)
    text_grad = ((grad_txt - txt_hat * txt_dot) * txt_inv).astype(jnp.bfloat16)
    weight_part = lax.dot_general(
        features, image_grad, (((0,), (0,)), ((), ())), preferred_element_type=jnp.float32
    )
    weight_grad = lax.psum(weight_part, "dp").astype(jnp.bfloat16)
    return (image_grad, text_grad, weight_grad)


def solution(mesh):
    in_specs = (P("dp", None), P(None, "rep"), P("dp", "rep"), P(), P())
    out_specs = (P("dp", "rep"), P("dp", "rep"), P(None, "rep"))
    return jax.shard_map(shards, mesh=mesh, in_specs=in_specs, out_specs=out_specs, check_vma=False)
```

profile of v0, /device:TPU:0, one launch (start us, length us, event | category | flops | bytes accessed | tf_op | source)
XLA Modules:
  0.0 178.6 jit_solution(2189384485302070662)
XLA Ops:
  0.6 1.2 fusion.34
  2.0 1.7 multiply_reduce_fusion.1
  3.7 5.8 %all-reduce.1 = (f32[256,1]{0,1:T(1,128)S(1)}, f32[256,1]{0,1:T(1,128)S(1)}) all-reduce(f32[256,1]{0,1:T(1,128)S(1)} %bitcast.54, f32[256,1]{0,1:T(1,128)S(1)} %bitcast.53), channel_id=1, replica_groups=mesh['dp'=16,'rep'=2] {'rep'}, use_global_device_ids=true, to_apply=%region_1.0 | all-reduce | flops 512 | bytes 4096 | tf_op jit(solution)/shard_map/psum | solution.py:24
  9.7 8.6 %all_gather.7 = bf16[256,1152]{0,1:T(8,128)(2,1)S(1)} all-gather(bf16[256,576]{0,1:T(8,128)(2,1)S(1)} %fusion.33), channel_id=1, replica_groups=mesh['dp'=16,'rep'=2] {'rep'}, dimensions={1}, use_global_device_ids=true | all-gather | bytes 884736 | tf_op jit(solution)/shard_map/all_gather | solution.py:39
  18.3 9.7 %all_gather.6 = bf16[256,1152]{0,1:T(8,128)(2,1)S(1)} all-gather(bf16[256,576]{0,1:T(8,128)(2,1)S(1)} %multiply_convert_fusion.1), channel_id=1, replica_groups=mesh['dp'=16,'rep'=2] {'rep'}, dimensions={1}, use_global_device_ids=true | all-gather | bytes 884736 | tf_op jit(solution)/shard_map/all_gather | solution.py:38
  30.0 1.1 collective-permute-start.4
  31.1 1.1 collective-permute-start.1
  32.7 9.4 %collective-permute-done.4 = bf16[256,1152]{0,1:T(8,128)(2,1)S(1)} collective-permute-done((bf16[256,1152]{0,1:T(8,128)(2,1)S(1)}, bf16[256,1152]{0,1:T(8,128)(2,1)S(1)}, u32[]{:S(2)}, u32[]{:S(2)}) %collective-permute-start.4) | collective-permute-done | bytes 589856 | tf_op jit(solution)/shard_map/ppermute | solution.py:14
  42.1 1.1 add_convert_fusion.3
  43.2 1.4 fusion.40
  44.6 3.9 %collective-permute-done.1 = bf16[256,1152]{0,1:T(8,128)(2,1)} collective-permute-done((bf16[256,1152]{0,1:T(8,128)(2,1)S(1)}, bf16[256,1152]{0,1:T(8,128)(2,1)}, u32[]{:S(2)}, u32[]{:S(2)}) %collective-permute-start.1) | collective-permute-done | bytes 589856 | tf_op jit(solution)/shard_map/ppermute | solution.py:14
  48.5 1.5 fusion.29
  50.3 5.2 %collective-permute-done.5 = bf16[256,1152]{0,1:T(8,128)(2,1)} collective-permute-done((bf16[256,1152]{0,1:T(8,128)(2,1)}, bf16[256,1152]{0,1:T(8,128)(2,1)}, u32[]{:S(2)}, u32[]{:S(2)}) %collective-permute-start.5) | collective-permute-done | bytes 589856 | tf_op jit(solution)/shard_map/ppermute | solution.py:14
  55.5 1.2 add_convert_fusion.2
  57.1 4.6 %collective-permute-done.2 = bf16[256,1152]{0,1:T(8,128)(2,1)S(1)} collective-permute-done((bf16[256,1152]{0,1:T(8,128)(2,1)}, bf16[256,1152]{0,1:T(8,128)(2,1)S(1)}, u32[]{:S(2)}, u32[]{:S(2)}) %collective-permute-start.2) | collective-permute-done | bytes 589856 | tf_op jit(solution)/shard_map/ppermute | solution.py:14
  62.5 6.3 %collective-permute-done.6 = bf16[256,1152]{0,1:T(8,128)(2,1)S(1)} collective-permute-done((bf16[256,1152]{0,1:T(8,128)(2,1)S(1)}, bf16[256,1152]{0,1:T(8,128)(2,1)S(1)}, u32[]{:S(2)}, u32[]{:S(2)}) %collective-permute-start.6) | collective-permute-done | bytes 589856 | tf_op jit(solution)/shard_map/ppermute | solution.py:14
  69.0 1.4 fusion.42
  70.4 4.7 %collective-permute-done.3 = bf16[256,1152]{0,1:T(8,128)(2,1)S(1)} collective-permute-done((bf16[256,1152]{0,1:T(8,128)(2,1)S(1)}, bf16[256,1152]{0,1:T(8,128)(2,1)S(1)}, u32[]{:S(2)}, u32[]{:S(2)}) %collective-permute-start.3) | collective-permute-done | bytes 589856 | tf_op jit(solution)/shard_map/ppermute | solution.py:14
  75.8 5.7 %collective-permute-done.7 = bf16[256,1152]{0,1:T(8,128)(2,1)S(1)} collective-permute-done((bf16[256,1152]{0,1:T(8,128)(2,1)S(1)}, bf16[256,1152]{0,1:T(8,128)(2,1)S(1)}, u32[]{:S(2)}, u32[]{:S(2)}) %collective-permute-start.7) | collective-permute-done | bytes 589856 | tf_op jit(solution)/shard_map/ppermute | solution.py:14
  83.3 0.9 copy-done.2
  84.4 8.8 %collective-permute-done.8 = bf16[256,1152]{0,1:T(8,128)(2,1)S(1)} collective-permute-done((bf16[256,1152]{0,1:T(8,128)(2,1)S(1)}, bf16[256,1152]{0,1:T(8,128)(2,1)S(1)}, u32[]{:S(2)}, u32[]{:S(2)}) %collective-permute-start.8) | collective-permute-done | bytes 589856 | tf_op jit(solution)/shard_map/ppermute | solution.py:14
  94.2 4.9 %all-reduce = (f32[256]{0:T(256)S(1)}, f32[256]{0:T(256)S(1)}) all-reduce(f32[256]{0:T(256)S(1)} %get-tuple-element.7, f32[256]{0:T(256)S(1)} %fusion.37), channel_id=1, replica_groups=mesh['dp'=16,'rep'=2] {'rep'}, use_global_device_ids=true, to_apply=%region_5.0 | all-reduce | flops 512 | bytes 4096 | tf_op jit(solution)/shard_map/psum | solution.py:67
  99.9 2.1 %convolution_bitcast_fusion = f32[1152,576]{0,1:T(8,128)} fusion(bf16[256,576]{0,1:T(8,128)(2,1)S(1)} %multiply_convert_fusion, bf16[256,1152]{1,0:T(8,128)(2,1)S(1)} %copy-done.3), kind=kOutput, calls=%fused_computation | convolution fusion | flops 339738624 | bytes 3538944 | tf_op jit(solution)/shard_map/dot_general | solution.py:76
  102.0 75.7 %all-reduce.3 = bf16[1152,576]{0,1:T(8,128)(2,1)} all-reduce(f32[1152,576]{0,1:T(8,128)} %convolution_bitcast_fusion), channel_id=1, replica_groups=mesh['dp'=16,'rep'=2] {'dp'}, use_global_device_ids=true, to_apply=%region_8.0 | all-reduce | flops 663552 | bytes 3981312 | tf_op jit(solution)/shard_map/psum | solution.py:79
  (42 shorter events, 8.5 us)
Async XLA Ops:
  0.6 1.4 copy-start
  2.0 7.6 %copy-start.1 = (bf16[256,576]{0,1:T(8,128)(2,1)S(1)}, bf16[256,576]{0,1:T(8,128)(2,1)}, u32[]{:S(2)}) copy-start(bf16[256,576]{0,1:T(8,128)(2,1)} %param.7) | copy-start | bytes 884740
  18.2 12.9 %collective-permute-start = (bf16[256,1152]{0,1:T(8,128)(2,1)S(1)}, bf16[256,1152]{0,1:T(8,128)(2,1)S(1)}, u32[]{:S(2)}, u32[]{:S(2)}) collective-permute-start(bf16[256,1152]{0,1:T(8,128)(2,1)S(1)} %all_gather.7), channel_id=1, source_target_pairs={{0,2},{2,4},{4,6},{6,8},{8,10},{10,12},{12,14},{14,16},{16,18},{18... | collective-permute-start | bytes 1769480 | tf_op jit(solution)/shard_map/ppermute | solution.py:14
  30.0 12.1 %collective-permute-start.4 = (bf16[256,1152]{0,1:T(8,128)(2,1)S(1)}, bf16[256,1152]{0,1:T(8,128)(2,1)S(1)}, u32[]{:S(2)}, u32[]{:S(2)}) collective-permute-start(bf16[256,1152]{0,1:T(8,128)(2,1)S(1)} %fusion), channel_id=1, source_target_pairs={{0,2},{2,4},{4,6},{6,8},{8,10},{10,12},{12,14},{14,16},{16,18},{18... | collective-permute-start | bytes 1769480 | tf_op jit(solution)/shard_map/ppermute | solution.py:14
  31.1 17.4 %collective-permute-start.1 = (bf16[256,1152]{0,1:T(8,128)(2,1)S(1)}, bf16[256,1152]{0,1:T(8,128)(2,1)}, u32[]{:S(2)}, u32[]{:S(2)}) collective-permute-start(bf16[256,1152]{0,1:T(8,128)(2,1)S(1)} %collective-permute-done), channel_id=1, source_target_pairs={{0,2},{2,4},{4,6},{6,8},{8,10},{10,12},{12,14},{14,16},{16,18},{18... | collective-permute-start | bytes 1769480 | tf_op jit(solution)/shard_map/ppermute | solution.py:14
  43.2 12.3 %collective-permute-start.5 = (bf16[256,1152]{0,1:T(8,128)(2,1)}, bf16[256,1152]{0,1:T(8,128)(2,1)}, u32[]{:S(2)}, u32[]{:S(2)}) collective-permute-start(bf16[256,1152]{0,1:T(8,128)(2,1)} %add_convert_fusion.3), channel_id=1, source_target_pairs={{0,2},{2,4},{4,6},{6,8},{8,10},{10,12},{12,14},{14,16},{16,18},{18... | collective-permute-start | bytes 1769480 | tf_op jit(solution)/shard_map/ppermute | solution.py:14
  48.5 13.2 %collective-permute-start.2 = (bf16[256,1152]{0,1:T(8,128)(2,1)}, bf16[256,1152]{0,1:T(8,128)(2,1)S(1)}, u32[]{:S(2)}, u32[]{:S(2)}) collective-permute-start(bf16[256,1152]{0,1:T(8,128)(2,1)} %collective-permute-done.1), channel_id=1, source_target_pairs={{0,2},{2,4},{4,6},{6,8},{8,10},{10,12},{12,14},{14,16},{16,18},{18... | collective-permute-start | bytes 1769480 | tf_op jit(solution)/shard_map/ppermute | solution.py:14
  56.7 12.1 %collective-permute-start.6 = (bf16[256,1152]{0,1:T(8,128)(2,1)S(1)}, bf16[256,1152]{0,1:T(8,128)(2,1)S(1)}, u32[]{:S(2)}, u32[]{:S(2)}) collective-permute-start(bf16[256,1152]{0,1:T(8,128)(2,1)S(1)} %add_convert_fusion.2), channel_id=1, source_target_pairs={{0,2},{2,4},{4,6},{6,8},{8,10},{10,12},{12,14},{14,16},{16,18},{18... | collective-permute-start | bytes 1769480 | tf_op jit(solution)/shard_map/ppermute | solution.py:14
  61.8 13.4 %collective-permute-start.3 = (bf16[256,1152]{0,1:T(8,128)(2,1)S(1)}, bf16[256,1152]{0,1:T(8,128)(2,1)S(1)}, u32[]{:S(2)}, u32[]{:S(2)}) collective-permute-start(bf16[256,1152]{0,1:T(8,128)(2,1)S(1)} %collective-permute-done.2), channel_id=1, source_target_pairs={{0,2},{2,4},{4,6},{6,8},{8,10},{10,12},{12,14},{14,16},{16,18},{18... | collective-permute-start | bytes 1769480 | tf_op jit(solution)/shard_map/ppermute | solution.py:14
  68.9 12.6 %collective-permute-start.7 = (bf16[256,1152]{0,1:T(8,128)(2,1)S(1)}, bf16[256,1152]{0,1:T(8,128)(2,1)S(1)}, u32[]{:S(2)}, u32[]{:S(2)}) collective-permute-start(bf16[256,1152]{0,1:T(8,128)(2,1)S(1)} %add_convert_fusion.1), channel_id=1, source_target_pairs={{0,2},{2,4},{4,6},{6,8},{8,10},{10,12},{12,14},{14,16},{16,18},{18... | collective-permute-start | bytes 1769480 | tf_op jit(solution)/shard_map/ppermute | solution.py:14
  81.7 11.6 %collective-permute-start.8 = (bf16[256,1152]{0,1:T(8,128)(2,1)S(1)}, bf16[256,1152]{0,1:T(8,128)(2,1)S(1)}, u32[]{:S(2)}, u32[]{:S(2)}) collective-permute-start(bf16[256,1152]{0,1:T(8,128)(2,1)S(1)} %add_convert_fusion), channel_id=1, source_target_pairs={{0,24},{2,26},{4,28},{6,30},{8,0},{10,2},{12,4},{14,6},{16,8},{18,... | collective-permute-start | bytes 1769480 | tf_op jit(solution)/shard_map/ppermute | solution.py:14
  82.9 1.3 copy-start.2
  84.4 15.5 %copy-start.3 = (bf16[256,1152]{1,0:T(8,128)(2,1)S(1)}, bf16[256,1152]{1,0:T(8,128)(2,1)}, u32[]{:S(2)}) copy-start(bf16[256,1152]{1,0:T(8,128)(2,1)} %param.5) | copy-start | bytes 1769476
  93.2 0.8 copy-start.5
  99.2 0.7 copy-start.4
  102.0 75.7 %copy-start.6 = (bf16[256,1152]{0,1:T(8,128)(2,1)S(1)}, bf16[256,1152]{0,1:T(8,128)(2,1)}, u32[]{:S(2)}) copy-start(bf16[256,1152]{0,1:T(8,128)(2,1)} %copy-done.5) | copy-start | bytes 1769476
where the time goes:
time: 179 us
  blocking collectives  105 us (59%)
  waiting for transfers between devices  48.7 us (27%)
  matrix products  13 us (7%)
  other arithmetic  4.1 us (2%)
  starting transfers between devices  3.24 us (2%)
  local copies, waits for them, and re-layouts  2.69 us (2%)
  between operations  2.14 us (1%)
    psum x1, blocking collectives, shards(): weight_grad = lax.psum(weight_part, 'dp').astype(jnp.bfloat16)  75.7 us
    ppermute x9, waiting for transfers between devices, passed_along(): lax.ppermute(array, axis, [(i, (i + by) % peers) for i in range(peers)])  48.7 us
    all_gather x1, blocking collectives, shards(): lax.all_gather(img_bf, 'rep', axis=1, tiled=True)  9.66 us
    all_gather x1, blocking collectives, shards(): lax.all_gather(txt_bf, 'rep', axis=1, tiled=True)  8.56 us
    psum x1, blocking collectives, shards(): lax.psum((jnp.sum(img_raw * img_raw, axis=1, keepdims=True), jnp.sum(txt_...  5.85 us
    psum x1, blocking collectives, shards(): lax.psum((jnp.sum(img_hat * grad_img, axis=1, keepdims=True), jnp.sum(txt...  4.93 us
    dot_general x5, matrix products, shards(): jnp.dot(grad_bf, text_span, preferred_element_type=jnp.float32)  3.8 us
  transfers between devices with their start and end apart: 9, of which 8 were waited for; matrix products, arithmetic and copies ran while one was open for 6% of the time, Pallas kernels for 0%

commit v1 on v0

v1 whole, which is shorter than its diff:
```python
import functools

import jax
import jax.numpy as jnp
from jax import lax
from jax.experimental import pallas as pl
from jax.experimental.pallas import tpu as pltpu
from jax.sharding import PartitionSpec as P

STEPS = 4
EPSILON = 1e-06
F32 = jnp.float32
BF16 = jnp.bfloat16
MESH = pl.DeviceIdType.MESH


def to_rows(first, second):
    n = first.shape[0]
    lane = lax.broadcasted_iota(jnp.int32, (n, 128), 1)
    return jnp.transpose(jnp.where(lane == 0, first, second))[:8]


def to_columns(rows):
    n = rows.shape[1]
    return jnp.transpose(jnp.concatenate([rows, jnp.zeros((120, n), F32)], axis=0))


def kernel(
    n, features, weight, text, log_scale, bias, img_out, txt_out, w_out,
    img_hat, img_bf, img_inv, txt_hat, txt_inv, span, d_img, d_txt, dots,
    own_score, score_out, score_in, back, from_core, sum_two, sum_four, two_in, four_in,
    feat_t, acc, half_out, half_in, quarter_out, quarter_in, eighth_out, eighth_in,
    last_out, last_in, rows_out, rows_in,
    s_span, r_span, s_score, r_score, s_back, r_back, s_w, r_w, s_rows, r_rows,
):
    k = lax.axis_index("dp")
    x = lax.axis_index("rep")
    tok = features.shape[0]
    part = weight.shape[1]
    odd = lax.rem(k, 2)
    high = lax.rem(k // 2, 2)

    def bit(b):
        return lax.rem(k // b, 2)

    def flip(b):
        return k + b - 2 * b * bit(b)

    def at(offset):
        return (lax.rem(k + offset + n, n), x)

    core = (flip(1), x)
    across = (k, 1 - x)
    far = []
    b = 8
    while b < n:
        far.append(b)
        b *= 2

    def copy(src, dst, s, r, device):
        return pltpu.make_async_remote_copy(
            src_ref=src, dst_ref=dst, send_sem=s, recv_sem=r,
            device_id=device, device_id_type=MESH,
        )

    barrier = pltpu.get_barrier_semaphore()
    friends = [across, core, at(2), at(-2), at(4), at(-4)] + [(flip(b), x) for b in far]
    for friend in friends:
        pl.semaphore_signal(barrier, inc=1, device_id=friend, device_id_type=MESH)

    raw = jnp.dot(features[...], weight[...], preferred_element_type=F32)
    txt_raw = text[...].astype(F32)
    sums = to_rows(
        jnp.sum(raw * raw, axis=1, keepdims=True),
        jnp.sum(txt_raw * txt_raw, axis=1, keepdims=True),
    )
    rows_out[0] = sums
    img_hat[...] = raw
    pl.semaphore_wait(barrier, len(friends))

    c = copy(rows_out.at[0], rows_in.at[0], s_rows.at[0], r_rows.at[0], across)
    c.start()
    feat_t[...] = jnp.transpose(features[...])
    c.wait()
    inverse = lax.rsqrt(to_columns(sums + rows_in[0]) + EPSILON)
    img_inv[...] = inverse[:, 0:1]
    txt_inv[...] = inverse[:, 1:2]
    hat = text[...].astype(F32) * txt_inv[...]
    txt_hat[...] = hat
    span[0] = hat.astype(BF16)

    own_four = copy(span.at[0], span.at[4], s_span.at[0], r_span.at[4], at(4))
    own_two = copy(span.at[0], span.at[2], s_span.at[1], r_span.at[2], at(2))
    pass_two = copy(span.at[4], span.at[2], s_span.at[1], r_span.at[2], at(-2))
    own_one = copy(span.at[0], span.at[1], s_span.at[2], r_span.at[1], core)
    pass_four = copy(span.at[4], span.at[3], s_span.at[2], r_span.at[3], core)
    slot = 3 - 2 * odd
    share_two = copy(span.at[2], span.at[slot], s_span.at[3], r_span.at[slot], core)

    own_four.start()

    @pl.when(high == 0)
    def _():
        own_two.start()

    @pl.when(odd == 0)
    def _():
        own_one.start()

    hat = img_hat[...] * img_inv[...]
    img_hat[...] = hat
    img_bf[...] = hat.astype(BF16)
    t_wide = jnp.exp(jnp.full((1, tok), log_scale[0], F32))
    t_part = jnp.exp(jnp.full((1, part), log_scale[0], F32))

    def arrived(s):
        copy(span.at[s], span.at[s], s_span.at[0], r_span.at[s], core).wait_recv()

    def score_copy(s):
        return copy(score_out.at[s], score_in.at[s], s_score.at[s], r_score.at[s], across)

    def begin(s):
        score = lax.dot_general(
            img_bf[...], span[s], (((1,), (1,)), ((), ())), preferred_element_type=F32
        )
        own_score[s] = score
        score_out[s] = score.astype(BF16)
        score_copy(s).start()

    def finish(s, first=False):
        score_copy(s).wait()
        score = own_score[s] + score_in[s].astype(F32)
        g = jax.nn.sigmoid(t_wide * score + bias[0])
        if s == 0:
            row = lax.broadcasted_iota(jnp.int32, (tok, tok), 0)
            col = lax.broadcasted_iota(jnp.int32, (tok, tok), 1)
            g = g - jnp.where(row == col, 1.0, 0.0)
        g = g.astype(BF16)
        dot = jnp.sum(g.astype(F32) * score, axis=1, keepdims=True)
        term = jnp.dot(g, span[s], preferred_element_type=F32)
        if first:
            d_img[...] = term
            dots[...] = dot
        else:
            d_img[...] += term
            dots[...] += dot
        return g

    def returned(g):
        return lax.dot_general(
            g, img_bf[...], (((0,), (0,)), ((), ())), preferred_element_type=F32
        )

    def core_copy(i):
        return copy(back.at[2 * i], from_core.at[i], s_back.at[i], r_back.at[i], core)

    begin(0)
    arrived(4)

    @pl.when(high == 1)
    def _():
        pass_two.start()

    @pl.when(odd == 1)
    def _():
        pass_four.start()

    begin(4)
    d_txt[...] = returned(finish(0, True))
    arrived(2)
    share_two.start()
    begin(2)
    back[3] = returned(finish(4)).astype(BF16)
    arrived(3)
    begin(3)
    back[1] = returned(finish(2)).astype(BF16)
    arrived(1)
    begin(1)
    back[2] = returned(finish(3)).astype(BF16)
    core_copy(1).start()
    g = finish(1)
    back[0] = returned(g).astype(BF16)
    core_copy(0).start()

    grad = ((d_img[...] - img_hat[...] * dots[...]) * t_part * img_inv[...]).astype(BF16)
    img_out[...] = grad

    depth = feat_t.shape[0]
    half, quarter, eighth = depth // 2, depth // 4, depth // 8

    def rows(start, size):
        return pl.ds(pl.multiple_of(start, 16), size)

    half_out[...] = jnp.dot(
        feat_t[rows((1 - odd) * half, half), :], img_out[...], preferred_element_type=F32
    ).astype(BF16)
    one = copy(half_out, half_in, s_w.at[0], r_w.at[0], core)
    one.start()
    acc[...] = jnp.dot(feat_t[rows(odd * half, half), :], img_out[...], preferred_element_type=F32)

    core_copy(0).wait_recv()
    core_copy(1).wait_recv()
    oddf = odd.astype(F32)
    highf = high.astype(F32)
    sum_two[...] = (back[1].astype(F32) + from_core[1 - odd].astype(F32)).astype(BF16)
    send_two = copy(sum_two, two_in, s_back.at[2], r_back.at[2], (flip(2), x))
    send_four = copy(sum_four, four_in, s_back.at[3], r_back.at[3], at(-4))

    first_b, second_b = 2 + 2 * odd, 4 - 2 * odd
    first_bit = high * (1 - odd) + bit(4) * odd
    second_bit = high * odd + bit(4) * (1 - odd)
    first_peer = (k + first_b - 2 * first_b * first_bit, x)
    second_peer = (k + second_b - 2 * second_b * second_bit, x)

    one.wait()
    acc[...] += half_in[...].astype(F32)
    quarter_out[...] = acc[rows((1 - first_bit) * quarter, quarter), :].astype(BF16)
    two = copy(quarter_out, quarter_in, s_w.at[1], r_w.at[1], first_peer)
    two.start()
    send_two.start()

    @pl.when(high == 0)
    def _():
        sum_four[...] = (back[3].astype(F32) + from_core[1].astype(F32) * oddf).astype(BF16)
        send_four.start()

    two.wait()
    keep = first_bit * quarter
    acc[rows(keep, quarter), :] += quarter_in[...].astype(F32)
    eighth_out[...] = acc[rows(keep + (1 - second_bit) * eighth, eighth), :].astype(BF16)
    three = copy(eighth_out, eighth_in, s_w.at[2], r_w.at[2], second_peer)
    three.start()

    send_two.wait()

    @pl.when(high == 1)
    def _():
        sum_four[...] = (
            back[3].astype(F32) + from_core[1].astype(F32) * oddf + two_in[...].astype(F32)
        ).astype(BF16)
        send_four.start()

    three.wait()
    keep = keep + second_bit * eighth
    total = acc[rows(keep, eighth), :] + eighth_in[...].astype(F32)
    for i, b in enumerate(far):
        last_out[i] = total.astype(BF16)
        c = copy(last_out.at[i], last_in.at[i], s_w.at[6 + i], r_w.at[6 + i], (flip(b), x))
        c.start()
        c.wait()
        total = last_out[i].astype(F32) + last_in[i].astype(F32)
    mine = odd * half + keep
    w_out[rows(mine, eighth), :] = total.astype(BF16)

    def spread(i, start, size, device):
        piece = w_out.at[rows(start, size), :]
        return copy(piece, piece, s_w.at[i], r_w.at[i], device)

    def landed(i, start, size):
        piece = w_out.at[rows(start, size), :]
        copy(piece, piece, s_w.at[i], r_w.at[i], core).wait_recv()

    c3 = spread(3, mine, eighth, second_peer)
    c3.start()

    send_four.wait()
    even = 1.0 - oddf
    grad = (
        d_txt[...] + four_in[...].astype(F32) + from_core[0].astype(F32) * even
        + two_in[...].astype(F32) * (1.0 - highf)
    )
    d_txt[...] = grad
    dot = jnp.sum(txt_hat[...] * grad, axis=1, keepdims=True)
    sums = to_rows(dot, dot)
    rows_out[1] = sums
    cd = copy(rows_out.at[1], rows_in.at[1], s_rows.at[1], r_rows.at[1], across)
    cd.start()

    quarter_at = odd * half + first_bit * quarter
    landed(3, quarter_at + (1 - second_bit) * eighth, eighth)
    c4 = spread(4, quarter_at, quarter, first_peer)
    c4.start()

    cd.wait()
    dot = to_columns(sums + rows_in[1])[:, 0:1]
    txt_out[...] = ((d_txt[...] - txt_hat[...] * dot) * t_part * txt_inv[...]).astype(BF16)

    landed(4, odd * half + (1 - first_bit) * quarter, quarter)
    c5 = spread(5, odd * half, half, core)
    c5.start()
    landed(5, (1 - odd) * half, half)

    c3.wait_send()
    c4.wait_send()
    c5.wait_send()
    own_four.wait_send()
    share_two.wait_send()
    core_copy(0).wait_send()
    core_copy(1).wait_send()

    @pl.when(high == 0)
    def _():
        own_two.wait_send()

    @pl.when(high == 1)
    def _():
        pass_two.wait_send()

    @pl.when(odd == 0)
    def _():
        own_one.wait_send()

    @pl.when(odd == 1)
    def _():
        pass_four.wait_send()


def shards(n, features, img_weight, text_embed, log_scale, logit_bias):
    tok, depth = features.shape
    part = img_weight.shape[1]
    vmem = pl.BlockSpec(memory_space=pltpu.VMEM)
    smem = pl.BlockSpec(memory_space=pltpu.SMEM)
    block = lambda dtype, *lead: pltpu.VMEM((*lead, tok, part), dtype)
    levels = 0
    while 8 << levels < n:
        levels += 1
    dma = pltpu.SemaphoreType.DMA
    pairs = STEPS + 1
    return pl.pallas_call(
        functools.partial(kernel, n),
        out_shape=(
            jax.ShapeDtypeStruct((tok, part), BF16),
            jax.ShapeDtypeStruct((tok, part), BF16),
            jax.ShapeDtypeStruct((depth, part), BF16),
        ),
        in_specs=[vmem, vmem, vmem, smem, smem],
        out_specs=(vmem, vmem, vmem),
        scratch_shapes=[
            block(F32), block(BF16), pltpu.VMEM((tok, 1), F32),
            block(F32), pltpu.VMEM((tok, 1), F32),
            block(BF16, pairs), block(F32), block(F32), pltpu.VMEM((tok, 1), F32),
            pltpu.VMEM((pairs, tok, tok), F32),
            pltpu.VMEM((pairs, tok, tok), BF16), pltpu.VMEM((pairs, tok, tok), BF16),
            block(BF16, 4), block(BF16, 2), block(BF16), block(BF16), block(BF16), block(BF16),
            pltpu.VMEM((depth, tok), BF16), pltpu.VMEM((depth // 2, part), F32),
            pltpu.VMEM((depth // 2, part), BF16), pltpu.VMEM((depth // 2, part), BF16),
            pltpu.VMEM((depth // 4, part), BF16), pltpu.VMEM((depth // 4, part), BF16),
            pltpu.VMEM((depth // 8, part), BF16), pltpu.VMEM((depth // 8, part), BF16),
            pltpu.VMEM((max(levels, 1), depth // 8, part), BF16),
            pltpu.VMEM((max(levels, 1), depth // 8, part), BF16),
            pltpu.VMEM((2, 8, tok), F32), pltpu.VMEM((2, 8, tok), F32),
            dma((4,)), dma((pairs,)), dma((pairs,)), dma((pairs,)), dma((4,)), dma((4,)),
            dma((6 + max(levels, 1),)), dma((6 + max(levels, 1),)), dma((2,)), dma((2,)),
        ],
        compiler_params=pltpu.CompilerParams(
            collective_id=0, has_side_effects=True, vmem_limit_bytes=48 * 1024 * 1024
        ),
    )(features, img_weight, text_embed, log_scale, logit_bias)


def solution(mesh):
    in_specs = (P("dp", None), P(None, "rep"), P("dp", "rep"), P(), P())
    out_specs = (P("dp", "rep"), P("dp", "rep"), P(None, "rep"))
    body = functools.partial(shards, mesh.shape["dp"])
    return jax.shard_map(body, mesh=mesh, in_specs=in_specs, out_specs=out_specs, check_vma=False)
```

time: 179 us -> 92.3 us (0.52)
  blocking collectives: 105 us -> 0 us
  Pallas kernels: 0 us -> 78.9 us
  waiting for transfers between devices: 48.7 us -> 0 us
  matrix products: 13 us -> 0 us
  local copies, waits for them, and re-layouts: 2.69 us -> 11.2 us
  other arithmetic: 4.1 us -> 0 us
  starting transfers between devices: 3.24 us -> 0 us
    psum x3 -> x0, blocking collectives: 86.5 us -> none  [the longest x1 75.7 us: shards(): weight_grad = lax.psum(weight_part, 'dp').astype(jnp.bfloat16)]
    pallas_call x0 -> x1, Pallas kernels: none -> 78.9 us  [shards(): pl.pallas_call(functools.partial(kernel, n), out_shape=(jax.ShapeDtypeStr...]
    ppermute x9 -> x0, waiting for transfers between devices: 48.7 us -> none  [passed_along(): lax.ppermute(array, axis, [(i, (i + by) % peers) for i in range(peers)])]
    all_gather x2 -> x0, blocking collectives: 18.2 us -> none  [the longest x1 9.66 us: shards(): lax.all_gather(img_bf, 'rep', axis=1, tiled=True)]
    dot_general x17 -> x0, matrix products: 13 us -> none  [the longest x5 3.8 us: shards(): jnp.dot(grad_bf, text_span, preferred_element_type=jnp.float32)]
    pallas_call x0 -> x3, local copies, waits for them, and re-layouts: none -> 5.43 us  [shards(): pl.pallas_call(functools.partial(kernel, n), out_shape=(jax.ShapeDtypeStr...]
    ppermute x9 -> x0, starting transfers between devices: 3.24 us -> none  [passed_along(): lax.ppermute(array, axis, [(i, (i + by) % peers) for i in range(peers)])]
    unnamed x14 -> x8, local copies, waits for them, and re-layouts: 2.69 us -> 5.74 us
  transfers between devices with their start and end apart: 9 -> 0, of which waited for: 8 -> 0; matrix products, arithmetic and copies ran while one was open for 6% -> 0% of each run, Pallas kernels for 0% -> 0%
where the time goes in v1:
time: 92.3 us; the launch traced here: 92 us
  Pallas kernels  78.9 us (85%)
  local copies, waits for them, and re-layouts  11.2 us (12%)
  between operations  1.96 us (2%)
    pallas_call x1, Pallas kernels, shards(): pl.pallas_call(functools.partial(kernel, n), out_shape=(jax.ShapeDtypeStr...  78.9 us
    unnamed x8, local copies, waits for them, and re-layouts  5.74 us
    pallas_call x3, local copies, waits for them, and re-layouts, shards(): pl.pallas_call(functools.partial(kernel, n), out_shape=(jax.ShapeDtypeStr...  5.43 us

profile of v1, /device:TPU:0, one launch (start us, length us, event | category | flops | bytes accessed | tf_op | source)
XLA Modules:
  0.0 92.0 jit_solution(16635588653886366832)
XLA Ops:
  1.9 1.2 %copy.9.text = bf16[256,576]{1,0:T(8,128)(2,1)S(1)} copy(bf16[256,576]{0,1:T(8,128)(2,1)} %param.7) | data formatting | bytes 589824 | tf_op args[2]
  3.1 2.1 %copy.8.weight = bf16[1152,576]{1,0:T(8,128)(2,1)S(1)} copy(bf16[1152,576]{0,1:T(8,128)(2,1)} %param.6) | data formatting | bytes 2654208 | tf_op args[1]
  5.2 0.0 copy-start
  5.2 1.1 %copy-done = bf16[256,1152]{1,0:T(8,128)(2,1)S(1)} copy-done((bf16[256,1152]{1,0:T(8,128)(2,1)S(1)}, bf16[256,1152]{1,0:T(8,128)(2,1)}, u32[]{:S(2)}) %copy-start) | copy-done | bytes 589848
  6.2 78.9 %shard_map.76 = (bf16[256,576]{1,0:T(8,128)(2,1)S(1)}, bf16[256,576]{1,0:T(8,128)(2,1)S(1)}, bf16[1152,576]{1,0:T(8,128)(2,1)S(1)}) custom-call(bf16[256,1152]{1,0:T(8,128)(2,1)S(1)} %copy-done, bf16[1152,576]{1,0:T(8,128)(2,1)S(1)} %copy.8.weight, bf16[256,576]{1,0:T(8,128)(2,1)S(1)} %copy.9.text, f32[1]{0:T(128)S(6)} %copy.13.log_scale, f32[1]{0:T(128)S(6)} %copy.14.bias), custom_call_target="tpu_custom_call" | custom-call | tf_op jit(solution)/shard_map/pallas_call | solution.py:329
  85.1 0.0 copy-start.1
  85.1 0.7 copy-done.1
  85.9 0.0 copy-start.2
  85.9 0.7 copy-done.2
  86.6 1.8 %copy.10 = bf16[256,576]{0,1:T(8,128)(2,1)} copy(bf16[256,576]{1,0:T(8,128)(2,1)} %copy-done.2) | data formatting | bytes 589824 | tf_op jit(solution)/shard_map/pallas_call | solution.py:329
  88.4 1.8 %copy.11 = bf16[256,576]{0,1:T(8,128)(2,1)} copy(bf16[256,576]{1,0:T(8,128)(2,1)} %copy-done.1) | data formatting | bytes 589824 | tf_op jit(solution)/shard_map/pallas_call | solution.py:329
  90.3 1.7 %copy.12 = bf16[1152,576]{0,1:T(8,128)(2,1)} copy(bf16[1152,576]{1,0:T(8,128)(2,1)S(1)} %get-tuple-element.5) | data formatting | bytes 2654208 | tf_op jit(solution)/shard_map/pallas_call | solution.py:329
Async XLA Ops:
  5.2 1.1 %copy-start = (bf16[256,1152]{1,0:T(8,128)(2,1)S(1)}, bf16[256,1152]{1,0:T(8,128)(2,1)}, u32[]{:S(2)}) copy-start(bf16[256,1152]{1,0:T(8,128)(2,1)} %features.1) | copy-start | bytes 1769476
  85.1 0.7 copy-start.1
  85.9 0.7 copy-start.2

commit v2 on v1

v2 whole, which is shorter than its diff:
```python
import functools

import jax
import jax.numpy as jnp
from jax import lax
from jax.experimental import pallas as pl
from jax.experimental.pallas import tpu as pltpu
from jax.sharding import PartitionSpec as P

STEPS = 4
CHUNKS = 2
TAIL = 16
EPSILON = 1e-06
F32 = jnp.float32
BF16 = jnp.bfloat16
MESH = pl.DeviceIdType.MESH


def kernel(
    n, features, weight, text, log_scale, bias, img_out, txt_out, w_out,
    img_hat, img_bf, img_rows, img_inv, span, squares, inverses, d_img, d_txt, dots,
    own_score, score_out, score_in, back, from_core, sum_two, sum_four, two_in, four_in,
    acc, half_out, half_in, quarter_out, quarter_in, eighth_out, eighth_in,
    last_out, last_in, rows_out, rows_in,
    s_span, r_span, s_score, r_score, s_back, r_back, s_w, r_w, s_rows, r_rows,
):
    k = lax.axis_index("dp")
    x = lax.axis_index("rep")
    tok = features.shape[0]
    part = weight.shape[0]
    odd = lax.rem(k, 2)
    high = lax.rem(k // 2, 2)

    def bit(b):
        return lax.rem(k // b, 2)

    def flip(b):
        return k + b - 2 * b * bit(b)

    def at(offset):
        return (lax.rem(k + offset + n, n), x)

    core = (flip(1), x)
    across = (k, 1 - x)
    far = []
    b = 8
    while b < n:
        far.append(b)
        b *= 2

    def copy(src, dst, s, r, device):
        return pltpu.make_async_remote_copy(
            src_ref=src, dst_ref=dst, send_sem=s, recv_sem=r,
            device_id=device, device_id_type=MESH,
        )

    barrier = pltpu.get_barrier_semaphore()
    friends = [across, core, at(2), at(-2), at(4), at(-4)] + [(flip(b), x) for b in far]
    for friend in friends:
        pl.semaphore_signal(barrier, inc=1, device_id=friend, device_id_type=MESH)
    pl.semaphore_wait(barrier, len(friends))

    size = part // CHUNKS

    def text_copy(source, target, c, device, i):
        piece = pl.ds(c * size, size)
        src = text if source is None else span.at[source]
        return copy(
            src.at[piece], span.at[target, piece], s_span.at[i, c], r_span.at[target, c], device
        )

    def arrived(s, c):
        piece = pl.ds(c * size, size)
        copy(
            span.at[s, piece], span.at[s, piece], s_span.at[0, c], r_span.at[s, c], core
        ).wait_recv()

    slot = 3 - 2 * odd
    own_four = [text_copy(None, 4, c, at(4), 0) for c in range(CHUNKS)]
    own_two = [text_copy(None, 2, c, at(2), 1) for c in range(CHUNKS)]
    pass_two = [text_copy(4, 2, c, at(-2), 1) for c in range(CHUNKS)]
    own_one = [text_copy(None, 1, c, core, 2) for c in range(CHUNKS)]
    pass_four = [text_copy(4, 3, c, core, 2) for c in range(CHUNKS)]
    share_two = [text_copy(2, slot, c, core, 3) for c in range(CHUNKS)]

    for c in range(CHUNKS):
        own_four[c].start()

        @pl.when(high == 0)
        def _():
            own_two[c].start()

        @pl.when(odd == 0)
        def _():
            own_one[c].start()

    def along(a, b):
        return lax.dot_general(a, b, (((1,), (1,)), ((), ())), preferred_element_type=F32)

    raw = along(weight[...], features[...])
    img_hat[...] = raw
    mine = jnp.sum(raw * raw, axis=0, keepdims=True)
    rows_out[0] = jnp.broadcast_to(mine, (8, tok))
    c = copy(rows_out.at[0], rows_in.at[0], s_rows.at[0], r_rows.at[0], across)
    c.start()
    t_wide = jnp.exp(jnp.full((1, tok), log_scale[0], F32))
    c.wait()
    inverse = lax.rsqrt(mine + rows_in[0, 0:1, :] + EPSILON)
    img_inv[...] = jnp.broadcast_to(inverse, (8, tok))
    hat = img_hat[...] * inverse
    img_hat[...] = hat
    img_bf[...] = hat.astype(BF16)
    img_rows[...] = jnp.transpose(img_bf[...])

    def text_of(s):
        return text[...] if s == 0 else span[s]

    def score_copy(s):
        return copy(score_out.at[s], score_in.at[s], s_score.at[s], r_score.at[s], across)

    def begin(s):
        block = text_of(s)
        score = jnp.dot(img_rows[...], block, preferred_element_type=F32)
        own_score[s] = score
        score_out[s, 0:tok, :] = score.astype(BF16)
        wide = block.astype(F32)
        square = jnp.sum(wide * wide, axis=0, keepdims=True)
        squares[s] = jnp.broadcast_to(square, (8, tok))
        top = square.astype(BF16).astype(F32)
        middle = (square - top).astype(BF16).astype(F32)
        low = square - top - middle
        row = lax.broadcasted_iota(jnp.int32, (TAIL, tok), 0)
        tail = jnp.where(row == 0, top, jnp.where(row == 1, middle, low))
        score_out[s, tok : tok + TAIL, :] = tail.astype(BF16)
        score_copy(s).start()

    def finish(s, first=False):
        score_copy(s).wait()
        tail = score_in[s, tok : tok + TAIL, :].astype(F32)
        square = squares[s, 0:1, :] + (tail[0:1] + tail[1:2] + tail[2:3])
        inverse = lax.rsqrt(square + EPSILON)
        if s == 0:
            inverses[...] = jnp.broadcast_to(inverse, (8, tok))
        score = (own_score[s] + score_in[s, 0:tok, :].astype(F32)) * inverse
        g = jax.nn.sigmoid(t_wide * score + bias[0])
        if s == 0:
            row = lax.broadcasted_iota(jnp.int32, (tok, tok), 0)
            col = lax.broadcasted_iota(jnp.int32, (tok, tok), 1)
            g = g - jnp.where(row == col, 1.0, 0.0)
        term = along(text_of(s), (g * inverse).astype(BF16))
        if first:
            d_img[...] = term
            dots[...] = g * score
        else:
            d_img[...] += term
            dots[...] += g * score
        return g.astype(BF16)

    def returned(g):
        return jnp.dot(img_bf[...], g, preferred_element_type=F32)

    def core_copy(i):
        return copy(back.at[2 * i], from_core.at[i], s_back.at[i], r_back.at[i], core)

    begin(0)
    for c in range(CHUNKS):
        arrived(4, c)

        @pl.when(high == 1)
        def _():
            pass_two[c].start()

        @pl.when(odd == 1)
        def _():
            pass_four[c].start()

    begin(4)
    d_txt[...] = returned(finish(0, True))
    for c in range(CHUNKS):
        arrived(2, c)
        share_two[c].start()
    begin(2)
    back[3] = returned(finish(4)).astype(BF16)
    for c in range(CHUNKS):
        arrived(3, c)
    begin(3)
    back[1] = returned(finish(2)).astype(BF16)
    for c in range(CHUNKS):
        arrived(1, c)
    begin(1)
    back[2] = returned(finish(3)).astype(BF16)
    core_copy(1).start()
    last_g = finish(1)

    dot = jnp.sum(jnp.transpose(dots[...]), axis=0, keepdims=True)
    grad = (d_img[...] - img_hat[...] * dot) * (t_wide * img_inv[0:1, :])
    img_out[...] = grad.astype(BF16)

    half, quarter = part // 2, part // 4
    eighth = (quarter // 2 + 15) // 16 * 16
    rest = quarter - eighth

    def rows(start, size):
        return pl.ds(pl.multiple_of(start, 16), size)

    half_out[...] = jnp.dot(
        img_out[rows((1 - odd) * half, half), :], features[...], preferred_element_type=F32
    ).astype(BF16)
    one = copy(half_out, half_in, s_w.at[0], r_w.at[0], core)
    one.start()
    back[0] = returned(last_g).astype(BF16)
    core_copy(0).start()
    acc[...] = jnp.dot(img_out[rows(odd * half, half), :], features[...], preferred_element_type=F32)

    oddf = odd.astype(F32)
    highf = high.astype(F32)
    send_two = copy(sum_two, two_in, s_back.at[2], r_back.at[2], (flip(2), x))
    send_four = copy(sum_four, four_in, s_back.at[3], r_back.at[3], at(-4))

    first_b, second_b = 2 + 2 * odd, 4 - 2 * odd
    first_bit = high * (1 - odd) + bit(4) * odd
    second_bit = high * odd + bit(4) * (1 - odd)
    first_peer = (k + first_b - 2 * first_b * first_bit, x)
    second_peer = (k + second_b - 2 * second_b * second_bit, x)

    one.wait()
    acc[...] += half_in[...].astype(F32)
    quarter_out[...] = acc[rows((1 - first_bit) * quarter, quarter), :].astype(BF16)
    two = copy(quarter_out, quarter_in, s_w.at[1], r_w.at[1], first_peer)
    two.start()

    core_copy(0).wait_recv()
    core_copy(1).wait_recv()
    sum_two[...] = (back[1].astype(F32) + from_core[1 - odd].astype(F32)).astype(BF16)

    two.wait()
    keep = first_bit * quarter
    acc[rows(keep, quarter), :] += quarter_in[...].astype(F32)
    eighth_out[...] = acc[rows(keep + (1 - second_bit) * rest, eighth), :].astype(BF16)
    three = copy(eighth_out, eighth_in, s_w.at[2], r_w.at[2], second_peer)
    three.start()
    three.wait()
    total = acc[rows(keep + second_bit * rest, eighth), :] + eighth_in[...].astype(F32)
    for i, b in enumerate(far):
        last_out[i] = total.astype(BF16)
        c = copy(last_out.at[i], last_in.at[i], s_w.at[6 + i], r_w.at[6 + i], (flip(b), x))
        c.start()
        if i == 0:
            send_two.start()
        c.wait()
        total = last_out[i].astype(F32) + last_in[i].astype(F32)
    last_out[0] = total.astype(BF16)
    base = odd * half + keep

    def spread(i, start, size, device):
        piece = w_out.at[rows(start, size), :]
        return copy(piece, piece, s_w.at[i], r_w.at[i], device)

    def landed(i, start, size):
        piece = w_out.at[rows(start, size), :]
        copy(piece, piece, s_w.at[i], r_w.at[i], core).wait_recv()

    @pl.when(second_bit == 0)
    def _():
        w_out[rows(base, eighth), :] = last_out[0]
        spread(3, base, eighth, second_peer).start()

    @pl.when(second_bit == 1)
    def _():
        w_out[rows(base + eighth, rest), :] = last_out[0, eighth - rest :, :]
        spread(3, base + eighth, rest, second_peer).start()

    @pl.when(high == 0)
    def _():
        sum_four[...] = (back[3].astype(F32) + from_core[1].astype(F32) * oddf).astype(BF16)
        send_four.start()

    @pl.when(second_bit == 0)
    def _():
        spread(3, base, eighth, second_peer).wait_send()
        landed(3, base + eighth, rest)

    @pl.when(second_bit == 1)
    def _():
        spread(3, base + eighth, rest, second_peer).wait_send()
        landed(3, base, eighth)

    c4 = spread(4, base, quarter, first_peer)
    c4.start()

    send_two.wait()

    @pl.when(high == 1)
    def _():
        sum_four[...] = (
            back[3].astype(F32) + from_core[1].astype(F32) * oddf + two_in[...].astype(F32)
        ).astype(BF16)
        send_four.start()

    landed(4, odd * half + (1 - first_bit) * quarter, quarter)
    c5 = spread(5, odd * half, half, core)
    c5.start()

    send_four.wait()
    even = 1.0 - oddf
    grad = (
        d_txt[...] + four_in[...].astype(F32) + from_core[0].astype(F32) * even
        + two_in[...].astype(F32) * (1.0 - highf)
    )
    d_txt[...] = grad
    hat = text[...].astype(F32) * inverses[0:1, :]
    dot = jnp.sum(hat * grad, axis=0, keepdims=True)
    rows_out[1] = jnp.broadcast_to(dot, (8, tok))
    cd = copy(rows_out.at[1], rows_in.at[1], s_rows.at[1], r_rows.at[1], across)
    cd.start()
    cd.wait()
    dot = dot + rows_in[1, 0:1, :]
    inverse = inverses[0:1, :]
    hat = text[...].astype(F32) * inverse
    txt_out[...] = ((d_txt[...] - hat * dot) * (t_wide * inverse)).astype(BF16)

    landed(5, (1 - odd) * half, half)
    c4.wait_send()
    c5.wait_send()
    core_copy(0).wait_send()
    core_copy(1).wait_send()
    for c in range(CHUNKS):
        own_four[c].wait_send()
        share_two[c].wait_send()

        @pl.when(high == 0)
        def _():
            own_two[c].wait_send()

        @pl.when(high == 1)
        def _():
            pass_two[c].wait_send()

        @pl.when(odd == 0)
        def _():
            own_one[c].wait_send()

        @pl.when(odd == 1)
        def _():
            pass_four[c].wait_send()


def shards(n, features, img_weight, text_embed, log_scale, logit_bias):
    tok, depth = features.shape
    part = img_weight.shape[1]
    vmem = pl.BlockSpec(memory_space=pltpu.VMEM)
    smem = pl.BlockSpec(memory_space=pltpu.SMEM)

    def block(dtype, *lead):
        return pltpu.VMEM((*lead, part, tok), dtype)

    def piece(size, dtype=BF16, *lead):
        return pltpu.VMEM((*lead, size, depth), dtype)

    levels = 1
    while 8 << levels < n:
        levels += 1
    dma = pltpu.SemaphoreType.DMA
    pairs = STEPS + 1
    half, quarter = part // 2, part // 4
    eighth = (quarter // 2 + 15) // 16 * 16
    row = pltpu.VMEM((8, tok), F32)
    img_grad, txt_grad, weight_grad = pl.pallas_call(
        functools.partial(kernel, n),
        out_shape=(
            jax.ShapeDtypeStruct((part, tok), BF16),
            jax.ShapeDtypeStruct((part, tok), BF16),
            jax.ShapeDtypeStruct((part, depth), BF16),
        ),
        in_specs=[vmem, vmem, vmem, smem, smem],
        out_specs=(vmem, vmem, vmem),
        scratch_shapes=[
            block(F32), block(BF16), pltpu.VMEM((tok, part), BF16), row,
            block(BF16, pairs), pltpu.VMEM((pairs, 8, tok), F32), row,
            block(F32), block(F32), pltpu.VMEM((tok, tok), F32),
            pltpu.VMEM((pairs, tok, tok), F32),
            pltpu.VMEM((pairs, tok + TAIL, tok), BF16), pltpu.VMEM((pairs, tok + TAIL, tok), BF16),
            block(BF16, 4), block(BF16, 2), block(BF16), block(BF16), block(BF16), block(BF16),
            piece(half, F32), piece(half), piece(half), piece(quarter), piece(quarter),
            piece(eighth), piece(eighth), piece(eighth, BF16, levels), piece(eighth, BF16, levels),
            pltpu.VMEM((2, 8, tok), F32), pltpu.VMEM((2, 8, tok), F32),
            dma((4, CHUNKS)), dma((pairs, CHUNKS)), dma((pairs,)), dma((pairs,)), dma((4,)), dma((4,)),
            dma((6 + levels,)), dma((6 + levels,)), dma((2,)), dma((2,)),
        ],
        compiler_params=pltpu.CompilerParams(
            collective_id=0, has_side_effects=True, vmem_limit_bytes=48 * 1024 * 1024
        ),
    )(features, img_weight.T, text_embed.T, log_scale, logit_bias)
    return img_grad.T, txt_grad.T, weight_grad.T


def solution(mesh):
    in_specs = (P("dp", None), P(None, "rep"), P("dp", "rep"), P(), P())
    out_specs = (P("dp", "rep"), P("dp", "rep"), P(None, "rep"))
    body = functools.partial(shards, mesh.shape["dp"])
    return jax.shard_map(body, mesh=mesh, in_specs=in_specs, out_specs=out_specs, check_vma=False)
```

time: 92.3 us -> 73.8 us (0.80)
  Pallas kernels: 78.9 us -> 64.8 us
  local copies, waits for them, and re-layouts: 11.2 us -> 5.83 us
    pallas_call x1, Pallas kernels: 78.9 us -> 64.8 us  [shards(): pl.pallas_call(functools.partial(kernel, n), out_shape=(jax.ShapeDtypeStr...]
    pallas_call x3 -> x0, local copies, waits for them, and re-layouts: 5.43 us -> none  [shards(): pl.pallas_call(functools.partial(kernel, n), out_shape=(jax.ShapeDtypeStr...]
    unnamed x8 -> x9, local copies, waits for them, and re-layouts: 5.74 us -> 5.83 us
where the time goes in v2:
time: 73.8 us; the launch traced here: 72.6 us
  Pallas kernels  64.8 us (88%)
  local copies, waits for them, and re-layouts  5.83 us (8%)
  between operations  1.94 us (3%)
    pallas_call x1, Pallas kernels, shards(): pl.pallas_call(functools.partial(kernel, n), out_shape=(jax.ShapeDtypeStr...  64.8 us
    unnamed x9, local copies, waits for them, and re-layouts  5.83 us

profile of v2, /device:TPU:0, one launch (start us, length us, event | category | flops | bytes accessed | tf_op | source)
XLA Modules:
  0.0 72.6 jit_solution(16527005768287165905)
XLA Ops:
  1.9 0.0 copy-start
  1.9 1.3 %copy-done = bf16[1152,576]{0,1:T(8,128)(2,1)S(1)} copy-done((bf16[1152,576]{0,1:T(8,128)(2,1)S(1)}, bf16[1152,576]{0,1:T(8,128)(2,1)}, u32[]{:S(2)}) %copy-start) | copy-done | bytes 1327128
  3.2 0.0 copy-start.1
  3.2 1.1 %copy-done.1 = bf16[256,1152]{1,0:T(8,128)(2,1)S(1)} copy-done((bf16[256,1152]{1,0:T(8,128)(2,1)S(1)}, bf16[256,1152]{1,0:T(8,128)(2,1)}, u32[]{:S(2)}) %copy-start.1) | copy-done | bytes 589848
  4.3 0.0 copy-start.2
  4.3 1.0 %copy-done.2 = bf16[256,576]{0,1:T(8,128)(2,1)S(1)} copy-done((bf16[256,576]{0,1:T(8,128)(2,1)S(1)}, bf16[256,576]{0,1:T(8,128)(2,1)}, u32[]{:S(2)}) %copy-start.2) | copy-done | bytes 294936
  5.3 64.8 %shard_map.76 = (bf16[576,256]{1,0:T(8,128)(2,1)S(1)}, bf16[576,256]{1,0:T(8,128)(2,1)S(1)}, bf16[576,1152]{1,0:T(8,128)(2,1)S(1)}) custom-call(bf16[256,1152]{1,0:T(8,128)(2,1)S(1)} %copy-done.1, bf16[576,1152]{1,0:T(8,128)(2,1)S(1)} %bitcast.5, bf16[576,256]{1,0:T(8,128)(2,1)S(1)} %bitcast.9, f32[1]{0:T(128)S(6)} %copy.11.log_scale, f32[1]{0:T(128)S(6)} %copy.12.bias), custom_call_target="tpu_custom_call" | custom-call | tf_op jit(solution)/shard_map/pallas_call | solution.py:368
  70.1 0.7 copy.13
  70.8 0.7 copy.14
  71.6 1.1 %copy.15 = bf16[1152,576]{0,1:T(8,128)(2,1)} copy(bf16[1152,576]{0,1:T(8,128)(2,1)S(1)} %bitcast.6) | data formatting | bytes 2654208
Async XLA Ops:
  1.9 1.3 %copy-start = (bf16[1152,576]{0,1:T(8,128)(2,1)S(1)}, bf16[1152,576]{0,1:T(8,128)(2,1)}, u32[]{:S(2)}) copy-start(bf16[1152,576]{0,1:T(8,128)(2,1)} %param.6) | copy-start | bytes 3981316
  3.2 1.1 %copy-start.1 = (bf16[256,1152]{1,0:T(8,128)(2,1)S(1)}, bf16[256,1152]{1,0:T(8,128)(2,1)}, u32[]{:S(2)}) copy-start(bf16[256,1152]{1,0:T(8,128)(2,1)} %features.1) | copy-start | bytes 1769476
  4.3 1.0 %copy-start.2 = (bf16[256,576]{0,1:T(8,128)(2,1)S(1)}, bf16[256,576]{0,1:T(8,128)(2,1)}, u32[]{:S(2)}) copy-start(bf16[256,576]{0,1:T(8,128)(2,1)} %param.7) | copy-start | bytes 884740

commit v3 on v2

--- a/solution.py
+++ b/solution.py
@@ -8,7 +8,7 @@
 from jax.sharding import PartitionSpec as P
 
 STEPS = 4
-CHUNKS = 2
+CHUNKS = 4
 TAIL = 16
 EPSILON = 1e-06
 F32 = jnp.float32
@@ -17,12 +17,13 @@
 
 
 def kernel(
-    n, features, weight, text, log_scale, bias, img_out, txt_out, w_out,
+    n, features_hbm, weight_hbm, text_hbm, log_scale, bias, img_out, txt_out, w_out,
+    features, weight, text,
     img_hat, img_bf, img_rows, img_inv, span, squares, inverses, d_img, d_txt, dots,
     own_score, score_out, score_in, back, from_core, sum_two, sum_four, two_in, four_in,
     acc, half_out, half_in, quarter_out, quarter_in, eighth_out, eighth_in,
     last_out, last_in, rows_out, rows_in,
-    s_span, r_span, s_score, r_score, s_back, r_back, s_w, r_w, s_rows, r_rows,
+    s_span, r_span, s_score, r_score, s_back, r_back, s_w, r_w, s_rows, r_rows, s_local,
 ):
     k = lax.axis_index("dp")
     x = lax.axis_index("rep")
@@ -54,6 +55,14 @@
             device_id=device, device_id_type=MESH,
         )
 
+    fetches = [
+        pltpu.make_async_copy(src, dst, s_local.at[i])
+        for i, (src, dst) in enumerate(
+            ((weight_hbm, weight), (features_hbm, features), (text_hbm, text))
+        )
+    ]
+    for fetch in fetches:
+        fetch.start()
     barrier = pltpu.get_barrier_semaphore()
     friends = [across, core, at(2), at(-2), at(4), at(-4)] + [(flip(b), x) for b in far]
     for friend in friends:
@@ -64,7 +73,7 @@
 
     def text_copy(source, target, c, device, i):
         piece = pl.ds(c * size, size)
-        src = text if source is None else span.at[source]
+        src = text_hbm if source is None else span.at[source]
         return copy(
             src.at[piece], span.at[target, piece], s_span.at[i, c], r_span.at[target, c], device
         )
@@ -97,6 +106,8 @@
     def along(a, b):
         return lax.dot_general(a, b, (((1,), (1,)), ((), ())), preferred_element_type=F32)
 
+    for fetch in fetches:
+        fetch.wait()
     raw = along(weight[...], features[...])
     img_hat[...] = raw
     mine = jnp.sum(raw * raw, axis=0, keepdims=True)
@@ -113,7 +124,7 @@
     img_rows[...] = jnp.transpose(img_bf[...])
 
     def text_of(s):
-        return text[...] if s == 0 else span[s]
+        return text[...] if isinstance(s, int) and s == 0 else span[s]
 
     def score_copy(s):
         return copy(score_out.at[s], score_in.at[s], s_score.at[s], r_score.at[s], across)
@@ -139,11 +150,11 @@
         tail = score_in[s, tok : tok + TAIL, :].astype(F32)
         square = squares[s, 0:1, :] + (tail[0:1] + tail[1:2] + tail[2:3])
         inverse = lax.rsqrt(square + EPSILON)
-        if s == 0:
+        if first:
             inverses[...] = jnp.broadcast_to(inverse, (8, tok))
         score = (own_score[s] + score_in[s, 0:tok, :].astype(F32)) * inverse
         g = jax.nn.sigmoid(t_wide * score + bias[0])
-        if s == 0:
+        if first:
             row = lax.broadcasted_iota(jnp.int32, (tok, tok), 0)
             col = lax.broadcasted_iota(jnp.int32, (tok, tok), 1)
             g = g - jnp.where(row == col, 1.0, 0.0)
@@ -162,35 +173,85 @@
     def core_copy(i):
         return copy(back.at[2 * i], from_core.at[i], s_back.at[i], r_back.at[i], core)
 
+    def choose(for_even, for_odd):
+        return for_even + odd * (for_odd - for_even)
+
+    oddf = odd.astype(F32)
+    highf = high.astype(F32)
+    send_two = copy(sum_two, two_in, s_back.at[2], r_back.at[2], (flip(2), x))
+    send_four = copy(sum_four, four_in, s_back.at[3], r_back.at[3], at(-4))
+    second, third, fifth = choose(4, 1), choose(3, 4), choose(1, 3)
+
     begin(0)
-    for c in range(CHUNKS):
-        arrived(4, c)
-
-        @pl.when(high == 1)
-        def _():
-            pass_two[c].start()
-
-        @pl.when(odd == 1)
-        def _():
+
+    @pl.when(odd == 1)
+    def _():
+        for c in range(CHUNKS):
+            arrived(1, c)
+
+    @pl.when(odd == 0)
+    def _():
+        for c in range(CHUNKS):
+            arrived(4, c)
+
+            @pl.when(high == 1)
+            def _():
+                pass_two[c].start()
+
+    begin(second)
+    d_txt[...] = returned(finish(0, True))
+
+    @pl.when(odd == 1)
+    def _():
+        for c in range(CHUNKS):
+            arrived(4, c)
             pass_four[c].start()
 
-    begin(4)
-    d_txt[...] = returned(finish(0, True))
+            @pl.when(high == 1)
+            def _():
+                pass_two[c].start()
+
+    @pl.when(odd == 0)
+    def _():
+        for c in range(CHUNKS):
+            arrived(3, c)
+
+    begin(third)
+    back[second - 1] = returned(finish(second)).astype(BF16)
+
+    @pl.when(odd == 1)
+    def _():
+        core_copy(0).start()
+
     for c in range(CHUNKS):
         arrived(2, c)
         share_two[c].start()
     begin(2)
-    back[3] = returned(finish(4)).astype(BF16)
+    back[third - 1] = returned(finish(third)).astype(BF16)
+
+    @pl.when(odd == 0)
+    def _():
+        core_copy(1).start()
+
     for c in range(CHUNKS):
-        arrived(3, c)
-    begin(3)
+        arrived(fifth, c)
+    begin(fifth)
     back[1] = returned(finish(2)).astype(BF16)
-    for c in range(CHUNKS):
-        arrived(1, c)
-    begin(1)
-    back[2] = returned(finish(3)).astype(BF16)
-    core_copy(1).start()
-    last_g = finish(1)
+
+    @pl.when(odd == 0)
+    def _():
+        sum_four[...] = back[3]
+
+    @pl.when(odd == 1)
+    def _():
+        core_copy(1).wait_recv()
+        sum_four[...] = (back[3].astype(F32) + from_core[1].astype(F32)).astype(BF16)
+
+    @pl.when(high == 0)
+    def _():
+        send_four.start()
+
+    last_g = finish(fifth)
 
     dot = jnp.sum(jnp.transpose(dots[...]), axis=0, keepdims=True)
     grad = (d_img[...] - img_hat[...] * dot) * (t_wide * img_inv[0:1, :])
@@ -208,14 +269,26 @@
     ).astype(BF16)
     one = copy(half_out, half_in, s_w.at[0], r_w.at[0], core)
     one.start()
-    back[0] = returned(last_g).astype(BF16)
-    core_copy(0).start()
+    back[fifth - 1] = returned(last_g).astype(BF16)
+
+    @pl.when(odd == 0)
+    def _():
+        core_copy(0).start()
+
+    @pl.when(odd == 1)
+    def _():
+        core_copy(1).start()
+
     acc[...] = jnp.dot(img_out[rows(odd * half, half), :], features[...], preferred_element_type=F32)
 
-    oddf = odd.astype(F32)
-    highf = high.astype(F32)
-    send_two = copy(sum_two, two_in, s_back.at[2], r_back.at[2], (flip(2), x))
-    send_four = copy(sum_four, four_in, s_back.at[3], r_back.at[3], at(-4))
+    core_copy(0).wait_recv()
+
+    @pl.when(odd == 0)
+    def _():
+        core_copy(1).wait_recv()
+
+    sum_two[...] = (back[1].astype(F32) + from_core[1 - odd].astype(F32)).astype(BF16)
+    send_two.start()
 
     first_b, second_b = 2 + 2 * odd, 4 - 2 * odd
     first_bit = high * (1 - odd) + bit(4) * odd
@@ -228,10 +301,6 @@
     quarter_out[...] = acc[rows((1 - first_bit) * quarter, quarter), :].astype(BF16)
     two = copy(quarter_out, quarter_in, s_w.at[1], r_w.at[1], first_peer)
     two.start()
-
-    core_copy(0).wait_recv()
-    core_copy(1).wait_recv()
-    sum_two[...] = (back[1].astype(F32) + from_core[1 - odd].astype(F32)).astype(BF16)
 
     two.wait()
     keep = first_bit * quarter
@@ -239,14 +308,21 @@
     eighth_out[...] = acc[rows(keep + (1 - second_bit) * rest, eighth), :].astype(BF16)
     three = copy(eighth_out, eighth_in, s_w.at[2], r_w.at[2], second_peer)
     three.start()
+    send_two.wait()
+
+    @pl.when(high == 1)
+    def _():
+        sum_four[...] = (
+            back[3].astype(F32) + from_core[1].astype(F32) * oddf + two_in[...].astype(F32)
+        ).astype(BF16)
+        send_four.start()
+
     three.wait()
     total = acc[rows(keep + second_bit * rest, eighth), :] + eighth_in[...].astype(F32)
     for i, b in enumerate(far):
         last_out[i] = total.astype(BF16)
         c = copy(last_out.at[i], last_in.at[i], s_w.at[6 + i], r_w.at[6 + i], (flip(b), x))
         c.start()
-        if i == 0:
-            send_two.start()
         c.wait()
         total = last_out[i].astype(F32) + last_in[i].astype(F32)
     last_out[0] = total.astype(BF16)
@@ -270,11 +346,6 @@
         w_out[rows(base + eighth, rest), :] = last_out[0, eighth - rest :, :]
         spread(3, base + eighth, rest, second_peer).start()
 
-    @pl.when(high == 0)
-    def _():
-        sum_four[...] = (back[3].astype(F32) + from_core[1].astype(F32) * oddf).astype(BF16)
-        send_four.start()
-
     @pl.when(second_bit == 0)
     def _():
         spread(3, base, eighth, second_peer).wait_send()
@@ -287,15 +358,6 @@
 
     c4 = spread(4, base, quarter, first_peer)
     c4.start()
-
-    send_two.wait()
-
-    @pl.when(high == 1)
-    def _():
-        sum_four[...] = (
-            back[3].astype(F32) + from_core[1].astype(F32) * oddf + two_in[...].astype(F32)
-        ).astype(BF16)
-        send_four.start()
 
     landed(4, odd * half + (1 - first_bit) * quarter, quarter)
     c5 = spread(5, odd * half, half, core)
@@ -349,6 +411,7 @@
     tok, depth = features.shape
     part = img_weight.shape[1]
     vmem = pl.BlockSpec(memory_space=pltpu.VMEM)
+    anywhere = pl.BlockSpec(memory_space=pl.ANY)
     smem = pl.BlockSpec(memory_space=pltpu.SMEM)
 
     def block(dtype, *lead):
@@ -372,9 +435,10 @@
             jax.ShapeDtypeStruct((part, tok), BF16),
             jax.ShapeDtypeStruct((part, depth), BF16),
         ),
-        in_specs=[vmem, vmem, vmem, smem, smem],
+        in_specs=[anywhere, anywhere, anywhere, smem, smem],
         out_specs=(vmem, vmem, vmem),
         scratch_shapes=[
+            pltpu.VMEM((tok, depth), BF16), piece(part), block(BF16),
             block(F32), block(BF16), pltpu.VMEM((tok, part), BF16), row,
             block(BF16, pairs), pltpu.VMEM((pairs, 8, tok), F32), row,
             block(F32), block(F32), pltpu.VMEM((tok, tok), F32),
@@ -385,10 +449,10 @@
             piece(eighth), piece(eighth), piece(eighth, BF16, levels), piece(eighth, BF16, levels),
             pltpu.VMEM((2, 8, tok), F32), pltpu.VMEM((2, 8, tok), F32),
             dma((4, CHUNKS)), dma((pairs, CHUNKS)), dma((pairs,)), dma((pairs,)), dma((4,)), dma((4,)),
-            dma((6 + levels,)), dma((6 + levels,)), dma((2,)), dma((2,)),
+            dma((6 + levels,)), dma((6 + levels,)), dma((2,)), dma((2,)), dma((3,)),
         ],
         compiler_params=pltpu.CompilerParams(
-            collective_id=0, has_side_effects=True, vmem_limit_bytes=48 * 1024 * 1024
+            collective_id=0, has_side_effects=True, vmem_limit_bytes=62 * 1024 * 1024
         ),
     )(features, img_weight.T, text_embed.T, log_scale, logit_bias)
     return img_grad.T, txt_grad.T, weight_grad.T

time: 73.8 us -> 82.9 us (1.12); the launches traced: 72.6 us -> 82.7 us
  Pallas kernels: 64.8 us -> 74.9 us
    pallas_call x1, Pallas kernels: 64.8 us -> 74.9 us  [shards(): pl.pallas_call(functools.partial(kernel, n), out_shape=(jax.ShapeDtypeStr...]
    unnamed x9 -> x3, local copies, waits for them, and re-layouts: 5.83 us -> 5.87 us
where the time goes in v3:
time: 82.9 us; the launch traced here: 82.7 us
  Pallas kernels  74.9 us (90%)
  local copies, waits for them, and re-layouts  5.87 us (7%)
  between operations  1.93 us (2%)
    pallas_call x1, Pallas kernels, shards(): pl.pallas_call(functools.partial(kernel, n), out_shape=(jax.ShapeDtypeStr...  74.9 us
    unnamed x3, local copies, waits for them, and re-layouts  5.87 us

profile of v3, /device:TPU:0, one launch (start us, length us, event | category | flops | bytes accessed | tf_op | source)
XLA Modules:
  0.0 82.7 jit_solution(15883029029986368632)
XLA Ops:
  1.9 74.9 %shard_map.76 = (bf16[576,256]{1,0:T(8,128)(2,1)}, bf16[576,256]{1,0:T(8,128)(2,1)}, bf16[576,1152]{1,0:T(8,128)(2,1)}) custom-call(bf16[256,1152]{1,0:T(8,128)(2,1)} %features_hbm.1, bf16[576,1152]{1,0:T(8,128)(2,1)} %bitcast.5, bf16[576,256]{1,0:T(8,128)(2,1)} %bitcast.9, f32[1]{0:T(128)S(6)} %copy.11.log_scale, f32[1]{0:T(128)S(6)} %copy.12.bias), custom_call_target="tpu_custom_call" | custom-call | tf_op jit(solution)/shard_map/pallas_call | solution.py:431
  76.8 1.7 %copy.13 = bf16[256,576]{0,1:T(8,128)(2,1)} copy(bf16[256,576]{0,1:T(8,128)(2,1)} %bitcast.8) | data formatting | bytes 589824
  78.5 1.7 %copy.14 = bf16[256,576]{0,1:T(8,128)(2,1)} copy(bf16[256,576]{0,1:T(8,128)(2,1)} %bitcast.7) | data formatting | bytes 589824
  80.2 2.5 %copy.15 = bf16[1152,576]{0,1:T(8,128)(2,1)} copy(bf16[1152,576]{0,1:T(8,128)(2,1)} %bitcast.6) | data formatting | bytes 2654208

commit v4 on v3

--- a/solution.py
+++ b/solution.py
@@ -21,7 +21,7 @@
     features, weight, text,
     img_hat, img_bf, img_rows, img_inv, span, squares, inverses, d_img, d_txt, dots,
     own_score, score_out, score_in, back, from_core, sum_two, sum_four, two_in, four_in,
-    acc, half_out, half_in, quarter_out, quarter_in, eighth_out, eighth_in,
+    acc, core_grad, core_features, quarter_out, quarter_in, eighth_out, eighth_in,
     last_out, last_in, rows_out, rows_in,
     s_span, r_span, s_score, r_score, s_back, r_back, s_w, r_w, s_rows, r_rows, s_local,
 ):
@@ -102,6 +102,9 @@
         @pl.when(odd == 0)
         def _():
             own_one[c].start()
+
+    core_features_copy = copy(features_hbm, core_features, s_rows.at[2], r_rows.at[2], core)
+    core_features_copy.start()
 
     def along(a, b):
         return lax.dot_general(a, b, (((1,), (1,)), ((), ())), preferred_element_type=F32)
@@ -260,15 +263,18 @@
     half, quarter = part // 2, part // 4
     eighth = (quarter // 2 + 15) // 16 * 16
     rest = quarter - eighth
+    depth = features.shape[1]
+    cut = (depth // 2 + 127) // 128 * 128
+    streams = (pl.ds(0, cut), pl.ds(cut, depth - cut))
+    both = range(2)
 
     def rows(start, size):
         return pl.ds(pl.multiple_of(start, 16), size)
 
-    half_out[...] = jnp.dot(
-        img_out[rows((1 - odd) * half, half), :], features[...], preferred_element_type=F32
-    ).astype(BF16)
-    one = copy(half_out, half_in, s_w.at[0], r_w.at[0], core)
-    one.start()
+    swap = copy(
+        img_out.at[rows((1 - odd) * half, half), :], core_grad, s_w.at[0], r_w.at[0], core
+    )
+    swap.start()
     back[fifth - 1] = returned(last_g).astype(BF16)
 
     @pl.when(odd == 0)
@@ -278,36 +284,65 @@
     @pl.when(odd == 1)
     def _():
         core_copy(1).start()
-
-    acc[...] = jnp.dot(img_out[rows(odd * half, half), :], features[...], preferred_element_type=F32)
-
-    core_copy(0).wait_recv()
-
-    @pl.when(odd == 0)
-    def _():
-        core_copy(1).wait_recv()
-
-    sum_two[...] = (back[1].astype(F32) + from_core[1 - odd].astype(F32)).astype(BF16)
-    send_two.start()
 
     first_b, second_b = 2 + 2 * odd, 4 - 2 * odd
     first_bit = high * (1 - odd) + bit(4) * odd
     second_bit = high * odd + bit(4) * (1 - odd)
     first_peer = (k + first_b - 2 * first_b * first_bit, x)
     second_peer = (k + second_b - 2 * second_b * second_bit, x)
-
-    one.wait()
-    acc[...] += half_in[...].astype(F32)
-    quarter_out[...] = acc[rows((1 - first_bit) * quarter, quarter), :].astype(BF16)
-    two = copy(quarter_out, quarter_in, s_w.at[1], r_w.at[1], first_peer)
-    two.start()
-
-    two.wait()
     keep = first_bit * quarter
-    acc[rows(keep, quarter), :] += quarter_in[...].astype(F32)
-    eighth_out[...] = acc[rows(keep + (1 - second_bit) * rest, eighth), :].astype(BF16)
-    three = copy(eighth_out, eighth_in, s_w.at[2], r_w.at[2], second_peer)
-    three.start()
+    mine_at = keep + second_bit * rest
+    base = odd * half + keep
+
+    def stage(i, u, src, dst, device):
+        lanes = streams[u]
+        return copy(
+            src.at[:, lanes], dst.at[:, lanes], s_w.at[1 + 2 * i + u], r_w.at[1 + 2 * i + u], device
+        )
+
+    acc[...] = jnp.dot(img_out[rows(odd * half, half), :], features[...], preferred_element_type=F32)
+    swap.wait()
+    core_features_copy.wait()
+    two, three = [], []
+    for u in both:
+        lanes = streams[u]
+        acc[:, lanes] += jnp.dot(
+            core_grad[...], core_features[:, lanes], preferred_element_type=F32
+        )
+        quarter_out[:, lanes] = acc[rows((1 - first_bit) * quarter, quarter), lanes].astype(BF16)
+        two.append(stage(0, u, quarter_out, quarter_in, first_peer))
+        two[u].start()
+
+    core_copy(0).wait_recv()
+
+    @pl.when(odd == 0)
+    def _():
+        core_copy(1).wait_recv()
+
+    sum_two[...] = (back[1].astype(F32) + from_core[1 - odd].astype(F32)).astype(BF16)
+    send_two.start()
+
+    for u in both:
+        lanes = streams[u]
+        two[u].wait()
+        acc[rows(keep, quarter), lanes] += quarter_in[:, lanes].astype(F32)
+        eighth_out[:, lanes] = acc[
+            rows(keep + (1 - second_bit) * rest, eighth), lanes
+        ].astype(BF16)
+        three.append(stage(1, u, eighth_out, eighth_in, second_peer))
+        three[u].start()
+
+    def exchange(i, u):
+        return stage(5 + i, u, last_out.at[i], last_in.at[i], (flip(far[i]), x))
+
+    for u in both:
+        lanes = streams[u]
+        three[u].wait()
+        total = acc[rows(mine_at, eighth), lanes] + eighth_in[:, lanes].astype(F32)
+        last_out[0, :, lanes] = total.astype(BF16)
+        if far:
+            exchange(0, u).start()
+
     send_two.wait()
 
     @pl.when(high == 1)
@@ -317,51 +352,49 @@
         ).astype(BF16)
         send_four.start()
 
-    three.wait()
-    total = acc[rows(keep + second_bit * rest, eighth), :] + eighth_in[...].astype(F32)
-    for i, b in enumerate(far):
-        last_out[i] = total.astype(BF16)
-        c = copy(last_out.at[i], last_in.at[i], s_w.at[6 + i], r_w.at[6 + i], (flip(b), x))
-        c.start()
-        c.wait()
-        total = last_out[i].astype(F32) + last_in[i].astype(F32)
-    last_out[0] = total.astype(BF16)
-    base = odd * half + keep
-
-    def spread(i, start, size, device):
-        piece = w_out.at[rows(start, size), :]
-        return copy(piece, piece, s_w.at[i], r_w.at[i], device)
-
-    def landed(i, start, size):
-        piece = w_out.at[rows(start, size), :]
-        copy(piece, piece, s_w.at[i], r_w.at[i], core).wait_recv()
-
-    @pl.when(second_bit == 0)
-    def _():
-        w_out[rows(base, eighth), :] = last_out[0]
-        spread(3, base, eighth, second_peer).start()
-
-    @pl.when(second_bit == 1)
-    def _():
-        w_out[rows(base + eighth, rest), :] = last_out[0, eighth - rest :, :]
-        spread(3, base + eighth, rest, second_peer).start()
-
-    @pl.when(second_bit == 0)
-    def _():
-        spread(3, base, eighth, second_peer).wait_send()
-        landed(3, base + eighth, rest)
-
-    @pl.when(second_bit == 1)
-    def _():
-        spread(3, base + eighth, rest, second_peer).wait_send()
-        landed(3, base, eighth)
-
-    c4 = spread(4, base, quarter, first_peer)
-    c4.start()
-
-    landed(4, odd * half + (1 - first_bit) * quarter, quarter)
-    c5 = spread(5, odd * half, half, core)
-    c5.start()
+    def spread(i, u, start, size, device):
+        piece = w_out.at[rows(start, size), streams[u]]
+        return copy(piece, piece, s_w.at[1 + 2 * i + u], r_w.at[1 + 2 * i + u], device)
+
+    for i in range(len(far)):
+        for u in both:
+            lanes = streams[u]
+            exchange(i, u).wait()
+            total = last_out[i, :, lanes].astype(F32) + last_in[i, :, lanes].astype(F32)
+            last_out[i + 1, :, lanes] = total.astype(BF16)
+            if i + 1 < len(far):
+                exchange(i + 1, u).start()
+
+    for u in both:
+        lanes = streams[u]
+
+        @pl.when(second_bit == 0)
+        def _():
+            w_out[rows(base, eighth), lanes] = last_out[len(far), :, lanes]
+            spread(2, u, base, eighth, second_peer).start()
+
+        @pl.when(second_bit == 1)
+        def _():
+            w_out[rows(base + eighth, rest), lanes] = last_out[len(far), eighth - rest :, lanes]
+            spread(2, u, base + eighth, rest, second_peer).start()
+
+    for u in both:
+
+        @pl.when(second_bit == 0)
+        def _():
+            spread(2, u, base, eighth, second_peer).wait_send()
+            spread(2, u, base + eighth, rest, second_peer).wait_recv()
+
+        @pl.when(second_bit == 1)
+        def _():
+            spread(2, u, base + eighth, rest, second_peer).wait_send()
+            spread(2, u, base, eighth, second_peer).wait_recv()
+
+        spread(3, u, base, quarter, first_peer).start()
+
+    for u in both:
+        spread(3, u, odd * half + (1 - first_bit) * quarter, quarter, first_peer).wait_recv()
+        spread(4, u, odd * half, half, core).start()
 
     send_four.wait()
     even = 1.0 - oddf
@@ -381,9 +414,10 @@
     hat = text[...].astype(F32) * inverse
     txt_out[...] = ((d_txt[...] - hat * dot) * (t_wide * inverse)).astype(BF16)
 
-    landed(5, (1 - odd) * half, half)
-    c4.wait_send()
-    c5.wait_send()
+    for u in both:
+        spread(4, u, (1 - odd) * half, half, core).wait_recv()
+        spread(3, u, base, quarter, first_peer).wait_send()
+        spread(4, u, odd * half, half, core).wait_send()
     core_copy(0).wait_send()
     core_copy(1).wait_send()
     for c in range(CHUNKS):
@@ -411,7 +445,7 @@
     tok, depth = features.shape
     part = img_weight.shape[1]
     vmem = pl.BlockSpec(memory_space=pltpu.VMEM)
-    anywhere = pl.BlockSpec(memory_space=pl.ANY)
+    anywhere = pl.BlockSpec(memory_space=pltpu.HBM)
     smem = pl.BlockSpec(memory_space=pltpu.SMEM)
 
     def block(dtype, *lead):
@@ -445,14 +479,14 @@
             pltpu.VMEM((pairs, tok, tok), F32),
             pltpu.VMEM((pairs, tok + TAIL, tok), BF16), pltpu.VMEM((pairs, tok + TAIL, tok), BF16),
             block(BF16, 4), block(BF16, 2), block(BF16), block(BF16), block(BF16), block(BF16),
-            piece(half, F32), piece(half), piece(half), piece(quarter), piece(quarter),
-            piece(eighth), piece(eighth), piece(eighth, BF16, levels), piece(eighth, BF16, levels),
+            piece(half, F32), pltpu.VMEM((half, tok), BF16), piece(tok), piece(quarter), piece(quarter),
+            piece(eighth), piece(eighth), piece(eighth, BF16, levels + 1), piece(eighth, BF16, levels),
             pltpu.VMEM((2, 8, tok), F32), pltpu.VMEM((2, 8, tok), F32),
             dma((4, CHUNKS)), dma((pairs, CHUNKS)), dma((pairs,)), dma((pairs,)), dma((4,)), dma((4,)),
-            dma((6 + levels,)), dma((6 + levels,)), dma((2,)), dma((2,)), dma((3,)),
+            dma((11 + 2 * levels,)), dma((11 + 2 * levels,)), dma((3,)), dma((3,)), dma((3,)),
         ],
         compiler_params=pltpu.CompilerParams(
-            collective_id=0, has_side_effects=True, vmem_limit_bytes=62 * 1024 * 1024
+            collective_id=0, has_side_effects=True, vmem_limit_bytes=48 * 1024 * 1024
         ),
     )(features, img_weight.T, text_embed.T, log_scale, logit_bias)
     return img_grad.T, txt_grad.T, weight_grad.T

time: 82.9 us -> 76.9 us (0.928)
  Pallas kernels: 74.9 us -> 68.9 us
    pallas_call x1, Pallas kernels: 74.9 us -> 68.9 us  [shards(): pl.pallas_call(functools.partial(kernel, n), out_shape=(jax.ShapeDtypeStr...]
    unnamed x3 -> x9, local copies, waits for them, and re-layouts: 5.87 us -> 5.83 us
where the time goes in v4:
time: 76.9 us; the launch traced here: 76.7 us
  Pallas kernels  68.9 us (90%)
  local copies, waits for them, and re-layouts  5.83 us (8%)
  between operations  1.94 us (3%)
    pallas_call x1, Pallas kernels, shards(): pl.pallas_call(functools.partial(kernel, n), out_shape=(jax.ShapeDtypeStr...  68.9 us
    unnamed x9, local copies, waits for them, and re-layouts  5.83 us

profile of v4, /device:TPU:0, one launch (start us, length us, event | category | flops | bytes accessed | tf_op | source)
XLA Modules:
  0.0 76.7 jit_solution(3537256400683162821)
XLA Ops:
  1.9 0.0 copy-start
  1.9 1.3 %copy-done = bf16[1152,576]{0,1:T(8,128)(2,1)S(1)} copy-done((bf16[1152,576]{0,1:T(8,128)(2,1)S(1)}, bf16[1152,576]{0,1:T(8,128)(2,1)}, u32[]{:S(2)}) %copy-start) | copy-done | bytes 1327128
  3.2 0.0 copy-start.1
  3.2 1.1 %copy-done.1 = bf16[256,1152]{1,0:T(8,128)(2,1)S(1)} copy-done((bf16[256,1152]{1,0:T(8,128)(2,1)S(1)}, bf16[256,1152]{1,0:T(8,128)(2,1)}, u32[]{:S(2)}) %copy-start.1) | copy-done | bytes 589848
  4.3 0.0 copy-start.2
  4.3 1.0 %copy-done.2 = bf16[256,576]{0,1:T(8,128)(2,1)S(1)} copy-done((bf16[256,576]{0,1:T(8,128)(2,1)S(1)}, bf16[256,576]{0,1:T(8,128)(2,1)}, u32[]{:S(2)}) %copy-start.2) | copy-done | bytes 294936
  5.3 68.9 %shard_map.76 = (bf16[576,256]{1,0:T(8,128)(2,1)S(1)}, bf16[576,256]{1,0:T(8,128)(2,1)S(1)}, bf16[576,1152]{1,0:T(8,128)(2,1)S(1)}) custom-call(bf16[256,1152]{1,0:T(8,128)(2,1)S(1)} %copy-done.1, bf16[576,1152]{1,0:T(8,128)(2,1)S(1)} %bitcast.5, bf16[576,256]{1,0:T(8,128)(2,1)S(1)} %bitcast.9, f32[1]{0:T(128)S(6)} %copy.11.log_scale, f32[1]{0:T(128)S(6)} %copy.12.bias), custom_call_target="tpu_custom_call" | custom-call | tf_op jit(solution)/shard_map/pallas_call | solution.py:465
  74.2 0.7 copy.13
  74.9 0.7 copy.14
  75.6 1.1 %copy.15 = bf16[1152,576]{0,1:T(8,128)(2,1)} copy(bf16[1152,576]{0,1:T(8,128)(2,1)S(1)} %bitcast.6) | data formatting | bytes 2654208
Async XLA Ops:
  1.9 1.3 %copy-start = (bf16[1152,576]{0,1:T(8,128)(2,1)S(1)}, bf16[1152,576]{0,1:T(8,128)(2,1)}, u32[]{:S(2)}) copy-start(bf16[1152,576]{0,1:T(8,128)(2,1)} %param.6) | copy-start | bytes 3981316
  3.2 1.1 %copy-start.1 = (bf16[256,1152]{1,0:T(8,128)(2,1)S(1)}, bf16[256,1152]{1,0:T(8,128)(2,1)}, u32[]{:S(2)}) copy-start(bf16[256,1152]{1,0:T(8,128)(2,1)} %features_hbm.1) | copy-start | bytes 1769476
  4.3 1.0 %copy-start.2 = (bf16[256,576]{0,1:T(8,128)(2,1)S(1)}, bf16[256,576]{0,1:T(8,128)(2,1)}, u32[]{:S(2)}) copy-start(bf16[256,576]{0,1:T(8,128)(2,1)} %param.7) | copy-start | bytes 884740

commit v5 on v4

--- a/solution.py
+++ b/solution.py
@@ -313,15 +313,6 @@
         two.append(stage(0, u, quarter_out, quarter_in, first_peer))
         two[u].start()
 
-    core_copy(0).wait_recv()
-
-    @pl.when(odd == 0)
-    def _():
-        core_copy(1).wait_recv()
-
-    sum_two[...] = (back[1].astype(F32) + from_core[1 - odd].astype(F32)).astype(BF16)
-    send_two.start()
-
     for u in both:
         lanes = streams[u]
         two[u].wait()
@@ -343,14 +334,14 @@
         if far:
             exchange(0, u).start()
 
-    send_two.wait()
-
-    @pl.when(high == 1)
-    def _():
-        sum_four[...] = (
-            back[3].astype(F32) + from_core[1].astype(F32) * oddf + two_in[...].astype(F32)
-        ).astype(BF16)
-        send_four.start()
+    core_copy(0).wait_recv()
+
+    @pl.when(odd == 0)
+    def _():
+        core_copy(1).wait_recv()
+
+    sum_two[...] = (back[1].astype(F32) + from_core[1 - odd].astype(F32)).astype(BF16)
+    send_two.start()
 
     def spread(i, u, start, size, device):
         piece = w_out.at[rows(start, size), streams[u]]
@@ -377,6 +368,15 @@
         def _():
             w_out[rows(base + eighth, rest), lanes] = last_out[len(far), eighth - rest :, lanes]
             spread(2, u, base + eighth, rest, second_peer).start()
+
+    send_two.wait()
+
+    @pl.when(high == 1)
+    def _():
+        sum_four[...] = (
+            back[3].astype(F32) + from_core[1].astype(F32) * oddf + two_in[...].astype(F32)
+        ).astype(BF16)
+        send_four.start()
 
     for u in both:
 
@@ -462,6 +462,10 @@
     half, quarter = part // 2, part // 4
     eighth = (quarter // 2 + 15) // 16 * 16
     row = pltpu.VMEM((8, tok), F32)
+    held = [
+        pltpu.with_memory_space_constraint(a, pltpu.HBM)
+        for a in (features, img_weight.T, text_embed.T)
+    ]
     img_grad, txt_grad, weight_grad = pl.pallas_call(
         functools.partial(kernel, n),
         out_shape=(
@@ -488,7 +492,7 @@
         compiler_params=pltpu.CompilerParams(
             collective_id=0, has_side_effects=True, vmem_limit_bytes=48 * 1024 * 1024
         ),
-    )(features, img_weight.T, text_embed.T, log_scale, logit_bias)
+    )(*held, log_scale, logit_bias)
     return img_grad.T, txt_grad.T, weight_grad.T
 
 

time: 76.9 us -> 67 us (0.87)
  the two profiles are of different devices: /device:TPU:0 before, /device:TPU:21 now
where the time goes in v5:
time: 67 us; the launch traced here: 66.8 us
  Pallas kernels  62.4 us (93%)
  local copies, waits for them, and re-layouts  2.49 us (4%)
  between operations  1.93 us (3%)
    pallas_call x1, Pallas kernels, shards(): pl.pallas_call(functools.partial(kernel, n), out_shape=(jax.ShapeDtypeStr...  62.4 us
    unnamed x3, local copies, waits for them, and re-layouts  2.49 us

profile of v5, /device:TPU:21, one launch (start us, length us, event | category | flops | bytes accessed | tf_op | source)
XLA Modules:
  0.0 66.8 jit_solution(2174343204245779014)
XLA Ops:
  1.9 62.4 %shard_map.76 = (bf16[576,256]{1,0:T(8,128)(2,1)S(1)}, bf16[576,256]{1,0:T(8,128)(2,1)S(1)}, bf16[576,1152]{1,0:T(8,128)(2,1)S(1)}) custom-call(bf16[256,1152]{1,0:T(8,128)(2,1)} %features_hbm.1, bf16[576,1152]{1,0:T(8,128)(2,1)} %bitcast.8, bf16[576,256]{1,0:T(8,128)(2,1)} %bitcast.9, f32[1]{0:T(128)S(6)} %copy.11.log_scale, f32[1]{0:T(128)S(6)} %copy.12.bias), custom_call_target="tpu_custom_call" | custom-call | tf_op jit(solution)/shard_map/pallas_call | solution.py:469
  64.4 0.7 %copy.13 = bf16[256,576]{0,1:T(8,128)(2,1)} copy(bf16[256,576]{0,1:T(8,128)(2,1)S(1)} %bitcast.7) | data formatting | bytes 589824
  65.1 0.7 %copy.14 = bf16[256,576]{0,1:T(8,128)(2,1)} copy(bf16[256,576]{0,1:T(8,128)(2,1)S(1)} %bitcast.6) | data formatting | bytes 589824
  65.8 1.1 %copy.15 = bf16[1152,576]{0,1:T(8,128)(2,1)} copy(bf16[1152,576]{0,1:T(8,128)(2,1)S(1)} %bitcast.5) | data formatting | bytes 2654208

commit v6 on v5

--- a/solution.py
+++ b/solution.py
@@ -104,7 +104,6 @@
             own_one[c].start()
 
     core_features_copy = copy(features_hbm, core_features, s_rows.at[2], r_rows.at[2], core)
-    core_features_copy.start()
 
     def along(a, b):
         return lax.dot_general(a, b, (((1,), (1,)), ((), ())), preferred_element_type=F32)
@@ -186,6 +185,7 @@
     second, third, fifth = choose(4, 1), choose(3, 4), choose(1, 3)
 
     begin(0)
+    core_features_copy.start()
 
     @pl.when(odd == 1)
     def _():
@@ -202,7 +202,6 @@
                 pass_two[c].start()
 
     begin(second)
-    d_txt[...] = returned(finish(0, True))
 
     @pl.when(odd == 1)
     def _():
@@ -213,6 +212,8 @@
             @pl.when(high == 1)
             def _():
                 pass_two[c].start()
+
+    d_txt[...] = returned(finish(0, True))
 
     @pl.when(odd == 0)
     def _():

time: 67 us -> 65.4 us (0.976)
  the two profiles are of different devices: /device:TPU:21 before, /device:TPU:0 now
where the time goes in v6:
time: 65.4 us; the launch traced here: 64.2 us
  Pallas kernels  59.8 us (91%)
  local copies, waits for them, and re-layouts  2.49 us (4%)
  between operations  1.93 us (3%)
    pallas_call x1, Pallas kernels, shards(): pl.pallas_call(functools.partial(kernel, n), out_shape=(jax.ShapeDtypeStr...  59.8 us
    unnamed x3, local copies, waits for them, and re-layouts  2.49 us

profile of v6, /device:TPU:0, one launch (start us, length us, event | category | flops | bytes accessed | tf_op | source)
XLA Modules:
  0.0 64.2 jit_solution(3816919081846933604)
XLA Ops:
  1.9 59.8 %shard_map.76 = (bf16[576,256]{1,0:T(8,128)(2,1)S(1)}, bf16[576,256]{1,0:T(8,128)(2,1)S(1)}, bf16[576,1152]{1,0:T(8,128)(2,1)S(1)}) custom-call(bf16[256,1152]{1,0:T(8,128)(2,1)} %features_hbm.1, bf16[576,1152]{1,0:T(8,128)(2,1)} %bitcast.8, bf16[576,256]{1,0:T(8,128)(2,1)} %bitcast.9, f32[1]{0:T(128)S(6)} %copy.11.log_scale, f32[1]{0:T(128)S(6)} %copy.12.bias), custom_call_target="tpu_custom_call" | custom-call | tf_op jit(solution)/shard_map/pallas_call | solution.py:470
  61.7 0.7 %copy.13 = bf16[256,576]{0,1:T(8,128)(2,1)} copy(bf16[256,576]{0,1:T(8,128)(2,1)S(1)} %bitcast.7) | data formatting | bytes 589824
  62.4 0.7 %copy.14 = bf16[256,576]{0,1:T(8,128)(2,1)} copy(bf16[256,576]{0,1:T(8,128)(2,1)S(1)} %bitcast.6) | data formatting | bytes 589824
  63.1 1.1 %copy.15 = bf16[1152,576]{0,1:T(8,128)(2,1)} copy(bf16[1152,576]{0,1:T(8,128)(2,1)S(1)} %bitcast.5) | data formatting | bytes 2654208

commit v7 on v6

--- a/solution.py
+++ b/solution.py
@@ -324,6 +324,15 @@
         three.append(stage(1, u, eighth_out, eighth_in, second_peer))
         three[u].start()
 
+    core_copy(0).wait_recv()
+
+    @pl.when(odd == 0)
+    def _():
+        core_copy(1).wait_recv()
+
+    sum_two[...] = (back[1].astype(F32) + from_core[1 - odd].astype(F32)).astype(BF16)
+    send_two.start()
+
     def exchange(i, u):
         return stage(5 + i, u, last_out.at[i], last_in.at[i], (flip(far[i]), x))
 
@@ -334,15 +343,6 @@
         last_out[0, :, lanes] = total.astype(BF16)
         if far:
             exchange(0, u).start()
-
-    core_copy(0).wait_recv()
-
-    @pl.when(odd == 0)
-    def _():
-        core_copy(1).wait_recv()
-
-    sum_two[...] = (back[1].astype(F32) + from_core[1 - odd].astype(F32)).astype(BF16)
-    send_two.start()
 
     def spread(i, u, start, size, device):
         piece = w_out.at[rows(start, size), streams[u]]

time: 65.4 us -> 65.4 us (level)
  no operation moved by 1% of the time
where the time goes in v7:
time: 65.4 us; the launch traced here: 64.2 us
  Pallas kernels  59.8 us (91%)
  local copies, waits for them, and re-layouts  2.49 us (4%)
  between operations  1.93 us (3%)
    pallas_call x1, Pallas kernels, shards(): pl.pallas_call(functools.partial(kernel, n), out_shape=(jax.ShapeDtypeStr...  59.8 us
    unnamed x3, local copies, waits for them, and re-layouts  2.49 us

profile of v7, /device:TPU:0, one launch (start us, length us, event | category | flops | bytes accessed | tf_op | source)
XLA Modules:
  0.0 64.2 jit_solution(13300348871356706698)
XLA Ops:
  1.9 59.8 %shard_map.76 = (bf16[576,256]{1,0:T(8,128)(2,1)S(1)}, bf16[576,256]{1,0:T(8,128)(2,1)S(1)}, bf16[576,1152]{1,0:T(8,128)(2,1)S(1)}) custom-call(bf16[256,1152]{1,0:T(8,128)(2,1)} %features_hbm.1, bf16[576,1152]{1,0:T(8,128)(2,1)} %bitcast.8, bf16[576,256]{1,0:T(8,128)(2,1)} %bitcast.9, f32[1]{0:T(128)S(6)} %copy.11.log_scale, f32[1]{0:T(128)S(6)} %copy.12.bias), custom_call_target="tpu_custom_call" | custom-call | tf_op jit(solution)/shard_map/pallas_call | solution.py:470
  61.7 0.7 %copy.13 = bf16[256,576]{0,1:T(8,128)(2,1)} copy(bf16[256,576]{0,1:T(8,128)(2,1)S(1)} %bitcast.7) | data formatting | bytes 589824
  62.4 0.7 %copy.14 = bf16[256,576]{0,1:T(8,128)(2,1)} copy(bf16[256,576]{0,1:T(8,128)(2,1)S(1)} %bitcast.6) | data formatting | bytes 589824
  63.1 1.1 %copy.15 = bf16[1152,576]{0,1:T(8,128)(2,1)} copy(bf16[1152,576]{0,1:T(8,128)(2,1)S(1)} %bitcast.5) | data formatting | bytes 2654208
